TPU v7x, 128 devices: a whole 4x4x4 slice. The times are simulated.
128 devices in a mesh: enc: 2 (over y_lo), ctx: 8 (over z, y_hi), tp: 8 (over x, core).
Axes of the slice: x: 4, y: 4 (y_hi: 2, y_lo: 2; y = y_hi * 2 + y_lo), z: 4, core: 2. Of those that a mesh axis runs over, the one named last changes fastest.
Arguments:
- query_rows: bfloat16 [12288, 6144], P(('enc', 'ctx', 'tp')), may hold values from -5 to 5
- key_rows: bfloat16 [12288, 6144], P(('enc', 'ctx', 'tp')), may hold values from -5 to 5
- value_rows: bfloat16 [12288, 6144], P(('enc', 'ctx', 'tp')), may hold values from -6 to 6
- out_grad: bfloat16 [12288, 6144], P(('enc', 'ctx', 'tp')), may hold values from -6 to 6
- clip_lengths: int32 [32], replicated, may hold values from 1 to 768, 12288 in all
Outputs:
- attended: bfloat16 [12288, 6144], P(('enc', 'ctx', 'tp'))
- query_grad: bfloat16 [12288, 6144], P(('enc', 'ctx', 'tp'))
- key_grad: bfloat16 [12288, 6144], P(('enc', 'ctx', 'tp'))
- value_grad: bfloat16 [12288, 6144], P(('enc', 'ctx', 'tp'))
Inputs may be any that keep to these rules, and one draw needn't show every extreme that they name: `clip_lengths`: clip lengths sum to 12288; the longest clip has exactly 768 tokens.
All inputs are finite; a program needn't handle non-finite values.
Results may differ from a plain program's by a relative error of at most 0.011.
Values may be sent and summed in bfloat16 or wider, within the bound.
No kernel may reach another device: no remote copies, remote signals or barrier semaphores. Data moves between devices by JAX's collectives and lax.ppermute only.
A program may use at most 128 MiB of HBM per device.

v0:
```python
import jax
import jax.numpy as jnp
from jax import lax
from jax.sharding import PartitionSpec as P

DH = 128


masked_score = -1e30


def padded(cells, sides, width):
    for axis, dim in sides:
        count = lax.axis_size(axis)
        ends = count - 1
        head = lax.slice_in_dim(cells, 0, width, axis=dim)
        tail = lax.slice_in_dim(cells, cells.shape[dim] - width, cells.shape[dim], axis=dim)
        cells = jnp.concatenate(
            [
                lax.ppermute(tail, axis, [(i, (i + 1) % count) for i in range(ends)]),
                cells,
                lax.ppermute(head, axis, [((i + 1) % count, i) for i in range(ends)]),
            ],
            axis=dim,
        )
    return cells


def from_behind(block, axis, distance):
    devices = range(lax.axis_size(axis))
    route = [(i - distance, i) for i in devices if i - distance in devices]
    return lax.ppermute(block, axis, route)


def clip_numbers(positions, clip_lengths):
    clip_ends = jnp.cumsum(clip_lengths)
    return jnp.sum((positions[:, None] >= clip_ends[None, :]).astype(jnp.int32), axis=1)


def window_pass(query_block, grad_block, key_window, value_window, allowed, score_scale):

    def single_head(items):
        query_one, grad_one, key_one, value_one = items
        scores = (
            jnp.einsum("id,jd->ij", query_one, key_one, preferred_element_type=jnp.float32)
            * score_scale
        )
        scores = jnp.where(allowed, scores, masked_score)
        top_score = jnp.max(scores, axis=1, keepdims=True)
        log_total = top_score + jnp.log(jnp.sum(jnp.exp(scores - top_score), axis=1, keepdims=True))
        prob_float = jnp.where(allowed, jnp.exp(scores - log_total), 0.0)
        prob_half = prob_float.astype(jnp.bfloat16)
        out_float = jnp.einsum(
            "ij,jd->id", prob_half, value_one, preferred_element_type=jnp.float32
        )
        correction = jnp.sum(grad_one.astype(jnp.float32) * out_float, axis=1)
        grad_prob = jnp.einsum("id,jd->ij", grad_one, value_one, preferred_element_type=jnp.float32)
        grad_score = (prob_float * (grad_prob - correction[:, None]) * score_scale).astype(
            jnp.bfloat16
        )
        query_part = jnp.einsum(
            "ij,jd->id", grad_score, key_one, preferred_element_type=jnp.float32
        ).astype(jnp.bfloat16)
        key_part = jnp.einsum(
            "ij,id->jd", grad_score, query_one, preferred_element_type=jnp.float32
        )
        value_part = jnp.einsum(
            "ij,id->jd", prob_half, grad_one, preferred_element_type=jnp.float32
        )
        return (out_float.astype(jnp.bfloat16), query_part, key_part, value_part)

    items = tuple(
        (jnp.moveaxis(array, 1, 0) for array in (query_block, grad_block, key_window, value_window))
    )
    results = lax.map(single_head, items)
    return tuple((jnp.moveaxis(array, 0, 1) for array in results))


def per_device(query_rows, key_rows, value_rows, out_grad, clip_lengths):
    query_local, key_local, value_local, grad_local = (
        lax.all_to_all(query_rows, "tp", split_axis=1, concat_axis=0, tiled=True),
        lax.all_to_all(key_rows, "tp", split_axis=1, concat_axis=0, tiled=True),
        lax.all_to_all(value_rows, "tp", split_axis=1, concat_axis=0, tiled=True),
        lax.all_to_all(out_grad, "tp", split_axis=1, concat_axis=0, tiled=True),
    )
    row_count, feature_count = query_local.shape
    head_count = feature_count // DH
    score_scale = DH ** (-0.5)
    shard_index = lax.axis_index(("enc", "ctx"))
    seq_total = row_count * lax.axis_size(("enc", "ctx"))
    positions = shard_index * row_count + jnp.arange(-row_count, 2 * row_count, dtype=jnp.int32)
    clip_ids = clip_numbers(positions, clip_lengths)
    inside = (positions >= 0) & (positions < seq_total)
    query_heads = query_local.reshape(row_count, head_count, DH)
    grad_heads = grad_local.reshape(row_count, head_count, DH)
    key_value = padded(jnp.stack((key_local, value_local)), ((("enc", "ctx"), 1),), row_count)
    key_window = key_value[0].reshape(3 * row_count, head_count, DH)
    value_window = key_value[1].reshape(3 * row_count, head_count, DH)
    own_ids = clip_ids[row_count : 2 * row_count]
    allowed = (own_ids[:, None] == clip_ids[None, :]) & inside[None, :]
    out_part, query_part, key_terms, value_terms = window_pass(
        query_heads, grad_heads, key_window, value_window, allowed, score_scale
    )
    lower_terms = jnp.stack((key_terms[:row_count], value_terms[:row_count]))
    upper_terms = jnp.stack((key_terms[2 * row_count :], value_terms[2 * row_count :]))
    from_above = from_behind(lower_terms, ("enc", "ctx"), -1)
    from_below = from_behind(upper_terms, ("enc", "ctx"), 1)
    key_total = key_terms[row_count : 2 * row_count] + from_above[0] + from_below[0]
    value_total = value_terms[row_count : 2 * row_count] + from_above[1] + from_below[1]
    attended_heads = out_part.reshape(row_count, feature_count)
    query_heads_grad = query_part.reshape(row_count, feature_count)
    key_heads_grad = key_total.astype(jnp.bfloat16).reshape(row_count, feature_count)
    value_heads_grad = value_total.astype(jnp.bfloat16).reshape(row_count, feature_count)
    attended, query_grad, key_grad, value_grad = (
        lax.all_to_all(attended_heads, "tp", split_axis=0, concat_axis=1, tiled=True),
        lax.all_to_all(query_heads_grad, "tp", split_axis=0, concat_axis=1, tiled=True),
        lax.all_to_all(key_heads_grad, "tp", split_axis=0, concat_axis=1, tiled=True),
        lax.all_to_all(value_heads_grad, "tp", split_axis=0, concat_axis=1, tiled=True),
    )
    return (attended, query_grad, key_grad, value_grad)


def solution(mesh):
    in_specs = (
        P(("enc", "ctx", "tp"), None),
        P(("enc", "ctx", "tp"), None),
        P(("enc", "ctx", "tp"), None),
        P(("enc", "ctx", "tp"), None),
        P(),
    )
    out_specs = (
        P(("enc", "ctx", "tp"), None),
        P(("enc", "ctx", "tp"), None),
        P(("enc", "ctx", "tp"), None),
        P(("enc", "ctx", "tp"), None),
    )
    return jax.shard_map(
        per_device, mesh=mesh, in_specs=in_specs, out_specs=out_specs, check_vma=False
    )
```

profile of v0, /device:TPU:96, one launch (start us, length us, event | category | flops | bytes accessed | tf_op | source)
XLA Modules:
  0.0 572.6 jit_solution(10973482092349016606)
XLA Ops:
  3.1 4.3 all-to-all-start.1
  7.5 17.3 %all-to-all-done.1 = bf16[96,8,768]{2,0,1:T(8,128)(2,1)S(1)} async-done(((bf16[96,8,768]{2,0,1:T(8,128)(2,1)}), bf16[96,8,768]{2,0,1:T(8,128)(2,1)S(1)}, u32[]{:S(2)}, u32[]{:S(2)}) %all-to-all-start.1) | async-done | bytes 1179680 | tf_op jit(solution)/shard_map/all_to_all | solution.py:82
  24.8 20.0 %all_to_all.140 = bf16[96,8,768]{2,0,1:T(8,128)(2,1)S(1)} all-to-all(bf16[96,8,768]{2,0,1:T(8,128)(2,1)S(1)} %bitcast.179), channel_id=1, replica_groups=mesh['enc'=2,'ctx'=8,'tp'=8] {'tp'}, dimensions={1} | all-to-all | bytes 2359296 | tf_op jit(solution)/shard_map/all_to_all | solution.py:83
  46.4 4.9 collective-permute-start.1
  54.9 3.7 all-to-all-start
  61.0 14.9 %all-to-all-done = bf16[96,8,768]{2,0,1:T(8,128)(2,1)S(1)} async-done(((bf16[96,8,768]{2,0,1:T(8,128)(2,1)}), bf16[96,8,768]{2,0,1:T(8,128)(2,1)S(1)}, u32[]{:S(2)}, u32[]{:S(2)}) %all-to-all-start) | async-done | bytes 1179680 | tf_op jit(solution)/shard_map/all_to_all | solution.py:81
  75.9 4.2 all-to-all-start.3
  86.0 2.6 copy.75
  88.5 9.0 %all-to-all-done.3 = bf16[96,8,768]{2,0,1:T(8,128)(2,1)} async-done(((bf16[96,8,768]{2,0,1:T(8,128)(2,1)}), bf16[96,8,768]{2,0,1:T(8,128)(2,1)}, u32[]{:S(2)}, u32[]{:S(2)}) %all-to-all-start.3) | async-done | bytes 1179680 | tf_op jit(solution)/shard_map/all_to_all | solution.py:84
  97.5 3.8 reshape.102
  101.3 2.7 copy.78
  103.9 49.4 %collective-permute-done = bf16[2,768,768]{2,1,0:T(8,128)(2,1)} collective-permute-done((bf16[2,768,768]{2,1,0:T(8,128)(2,1)}, bf16[2,768,768]{2,1,0:T(8,128)(2,1)}, u32[]{:S(2)}, u32[]{:S(2)}) %collective-permute-start) | collective-permute-done | bytes 2359328 | tf_op jit(solution)/shard_map/ppermute | solution.py:20
  153.3 3.2 pad_maximum_fusion
  158.8 5.8 %copy.71 = bf16[1,2304,768]{1,2,0:T(8,128)(2,1)} copy(bf16[1,2304,768]{2,1,0:T(8,128)(2,1)} %get-tuple-element.186) | data formatting | bytes 7077888 | tf_op jit(solution)/shard_map/slice | solution.py:98
  164.5 4.0 copy.70
  168.6 136.0 %while.17 = (s32[]{:T(128)}, bf16[6,768,128]{1,2,0:T(8,128)(2,1)}, bf16[6,768,128]{2,1,0:T(8,128)(2,1)}, f32[6,2304,128]{2,1,0:T(8,128)}, f32[6,2304,128]{2,1,0:...) while((s32[]{:T(128)}, bf16[6,768,128]{1,2,0:T(8,128)(2,1)}, ...), condition=%wide.region_6.7_spmd.clone, body=%wide.region_2.6_spmd.clone.sunk | while | flops 2753788416 | bytes 61242816 | solution.py:75
  168.6 3.1 fusion.65
  172.8 2.6 fusion.66
  175.3 3.1 bitcast_dynamic-update-slice_fusion.2
  178.5 4.6 multiply_convert_fusion.2
  183.1 2.8 fusion.67
  185.9 3.1 fusion.68
  191.2 3.1 fusion.65
  195.4 2.6 fusion.66
  198.0 3.1 bitcast_dynamic-update-slice_fusion.2
  201.2 4.6 multiply_convert_fusion.2
  205.8 2.8 fusion.67
  208.6 3.1 fusion.68
  213.9 3.1 fusion.65
  218.2 2.6 fusion.66
  220.7 3.1 bitcast_dynamic-update-slice_fusion.2
  223.9 4.6 multiply_convert_fusion.2
  228.5 2.8 fusion.67
  231.3 3.1 fusion.68
  236.6 3.1 fusion.65
  240.8 2.6 fusion.66
  243.4 3.1 bitcast_dynamic-update-slice_fusion.2
  246.6 4.6 multiply_convert_fusion.2
  251.2 2.8 fusion.67
  254.0 3.1 fusion.68
  259.2 3.1 fusion.65
  263.5 2.6 fusion.66
  266.0 3.1 bitcast_dynamic-update-slice_fusion.2
  269.2 4.6 multiply_convert_fusion.2
  273.8 2.8 fusion.67
  276.6 3.1 fusion.68
  281.9 3.1 fusion.65
  286.2 2.6 fusion.66
  288.7 3.1 bitcast_dynamic-update-slice_fusion.2
  291.9 4.6 multiply_convert_fusion.2
  296.5 2.8 fusion.67
  299.3 3.1 fusion.68
  304.6 4.4 slice_bitcast_fusion.6
  311.6 5.9 %collective-permute-start.3 = (f32[2,768,6,128]{3,1,2,0:T(8,128)}, f32[2,768,6,128]{3,1,2,0:T(8,128)}, u32[]{:S(2)}, u32[]{:S(2)}) collective-permute-start(f32[2,768,6,128]{3,1,2,0:T(8,128)} %pad_maximum_fusion.2), channel_id=1, source_target_pairs={{0,8},{8,16},{16,24},{24,32},{32,40},{40,48},{48,56},{56,64},{64,7... | collective-permute-start | bytes 14155784 | tf_op jit(solution)/shard_map/ppermute | solution.py:32
  326.0 3.6 all-to-all-start.4
  333.8 13.0 %all-to-all-done.4 = bf16[8,96,768]{2,1,0:T(8,128)(2,1)S(1)} async-done(((bf16[8,96,768]{2,1,0:T(8,128)(2,1)}), bf16[8,96,768]{2,1,0:T(8,128)(2,1)S(1)}, u32[]{:S(2)}, u32[]{:S(2)}) %all-to-all-start.4) | async-done | bytes 1179680 | tf_op jit(solution)/shard_map/all_to_all | solution.py:115
  346.8 4.2 all-to-all-start.5
  351.1 69.8 %collective-permute-done.3 = f32[2,768,6,128]{3,1,2,0:T(8,128)} collective-permute-done((f32[2,768,6,128]{3,1,2,0:T(8,128)}, f32[2,768,6,128]{3,1,2,0:T(8,128)}, u32[]{:S(2)}, u32[]{:S(2)}) %collective-permute-start.3) | collective-permute-done | bytes 4718624 | tf_op jit(solution)/shard_map/ppermute | solution.py:32
  420.9 99.2 %collective-permute-done.2 = f32[2,768,6,128]{3,1,2,0:T(8,128)} collective-permute-done((f32[2,768,6,128]{3,1,2,0:T(8,128)}, f32[2,768,6,128]{3,1,2,0:T(8,128)}, u32[]{:S(2)}, u32[]{:S(2)}) %collective-permute-start.2) | collective-permute-done | bytes 4718624 | tf_op jit(solution)/shard_map/ppermute | solution.py:32
  520.1 5.8 %fusion.31 = (bf16[768,6,128]{2,0,1:T(8,128)(2,1)S(1)}, bf16[768,6,128]{2,0,1:T(8,128)(2,1)S(1)}) fusion(f32[2,768,6,128]{3,1,2,0:T(8,128)} %collective-permute-done.3, f32[2,768,6,128]{3,1,2,0:T(8,128)} %collective-permute-done.2, f32[2304,6,128]{2,0,1:T(8,128)} %bitcast.172, f32[2304,6,128]{2,0,1:T(8,128)} %bitcast.174), kind=kLoop, calls=%fused_computation.45 | loop fusion | flops 3538944 | bytes 16515072 | tf_op jit(solution)/shard_map/convert_element_type | solution.py:113
  528.9 4.3 all-to-all-start.7
  536.3 14.3 %all-to-all-done.7 = bf16[8,96,768]{2,1,0:T(8,128)(2,1)} async-done(((bf16[8,96,768]{2,1,0:T(8,128)(2,1)}), bf16[8,96,768]{2,1,0:T(8,128)(2,1)}, u32[]{:S(2)}, u32[]{:S(2)}) %all-to-all-start.7) | async-done | bytes 1179680 | tf_op jit(solution)/shard_map/all_to_all | solution.py:118
  550.6 3.6 all-to-all-start.6
  560.1 11.4 %all-to-all-done.6 = bf16[8,96,768]{2,1,0:T(8,128)(2,1)S(1)} async-done(((bf16[8,96,768]{2,1,0:T(8,128)(2,1)}), bf16[8,96,768]{2,1,0:T(8,128)(2,1)S(1)}, u32[]{:S(2)}, u32[]{:S(2)}) %all-to-all-start.6) | async-done | bytes 1179680 | tf_op jit(solution)/shard_map/all_to_all | solution.py:117
  (96 shorter events, 66.6 us)
Async XLA Ops:
  0.6 6.8 %copy-start.3 = (bf16[96,6144]{1,0:T(8,128)(2,1)S(1)}, bf16[96,6144]{1,0:T(8,128)(2,1)}, u32[]{:S(2)}) copy-start(bf16[96,6144]{1,0:T(8,128)(2,1)} %param.9) | copy-start | bytes 3538948
  3.1 21.7 %all-to-all-start.1 = ((bf16[96,8,768]{2,0,1:T(8,128)(2,1)}), bf16[96,8,768]{2,0,1:T(8,128)(2,1)S(1)}, u32[]{:S(2)}, u32[]{:S(2)}) async-start(bf16[96,8,768]{2,0,1:T(8,128)(2,1)} %bitcast.130), calls=%async_computation.1 | async-start | bytes 2359296 | tf_op jit(solution)/shard_map/all_to_all | solution.py:82
  24.8 29.0 %copy-start.4 = (bf16[96,6144]{1,0:T(8,128)(2,1)S(1)}, bf16[96,6144]{1,0:T(8,128)(2,1)}, u32[]{:S(2)}) copy-start(bf16[96,6144]{1,0:T(8,128)(2,1)} %param.7) | copy-start | bytes 3538948
  46.4 57.5 %collective-permute-start.1 = (bf16[2,768,768]{2,1,0:T(8,128)(2,1)}, bf16[2,768,768]{2,1,0:T(8,128)(2,1)}, u32[]{:S(2)}, u32[]{:S(2)}) collective-permute-start(bf16[2,768,768]{2,1,0:T(8,128)(2,1)} %pad_maximum_fusion.3), channel_id=1, source_target_pairs={{8,0},{16,8},{24,16},{32,24},{40,32},{48,40},{56,48},{64,56},{72,6... | collective-permute-start | bytes 7077896 | tf_op jit(solution)/shard_map/ppermute | solution.py:22
  51.4 102.0 %collective-permute-start = (bf16[2,768,768]{2,1,0:T(8,128)(2,1)}, bf16[2,768,768]{2,1,0:T(8,128)(2,1)}, u32[]{:S(2)}, u32[]{:S(2)}) collective-permute-start(bf16[2,768,768]{2,1,0:T(8,128)(2,1)} %pad_maximum_fusion.3), channel_id=1, source_target_pairs={{0,8},{8,16},{16,24},{24,32},{32,40},{40,48},{48,56},{56,64},{64,7... | collective-permute-start | bytes 7077896 | tf_op jit(solution)/shard_map/ppermute | solution.py:20
  54.9 25.3 %copy-start.7 = (s32[32]{0:T(128)S(1)}, s32[32]{0:T(128)}, u32[]{:S(2)}) copy-start(s32[32]{0:T(128)} %param.11) | copy-start | bytes 388
  54.9 21.0 %all-to-all-start = ((bf16[96,8,768]{2,0,1:T(8,128)(2,1)}), bf16[96,8,768]{2,0,1:T(8,128)(2,1)S(1)}, u32[]{:S(2)}, u32[]{:S(2)}) async-start(bf16[96,8,768]{2,0,1:T(8,128)(2,1)} %bitcast.131), calls=%async_computation | async-start | bytes 2359296 | tf_op jit(solution)/shard_map/all_to_all | solution.py:81
  75.9 21.6 %all-to-all-start.3 = ((bf16[96,8,768]{2,0,1:T(8,128)(2,1)}), bf16[96,8,768]{2,0,1:T(8,128)(2,1)}, u32[]{:S(2)}, u32[]{:S(2)}) async-start(bf16[96,8,768]{2,0,1:T(8,128)(2,1)} %bitcast.128), calls=%async_computation.3 | async-start | bytes 2359296 | tf_op jit(solution)/shard_map/all_to_all | solution.py:84
  171.6 1.1 copy-start.6
  175.3 3.1 copy-start
  194.3 1.1 copy-start.6
  198.0 3.1 copy-start
  217.0 1.1 copy-start.6
  220.7 3.1 copy-start
  239.7 1.1 copy-start.6
  243.4 3.1 copy-start
  262.3 1.1 copy-start.6
  266.0 3.1 copy-start
  285.0 1.1 copy-start.6
  288.7 3.1 copy-start
  311.6 109.3 %collective-permute-start.3 = (f32[2,768,6,128]{3,1,2,0:T(8,128)}, f32[2,768,6,128]{3,1,2,0:T(8,128)}, u32[]{:S(2)}, u32[]{:S(2)}) collective-permute-start(f32[2,768,6,128]{3,1,2,0:T(8,128)} %pad_maximum_fusion.2), channel_id=1, source_target_pairs={{0,8},{8,16},{16,24},{24,32},{32,40},{40,48},{48,56},{56,64},{64,7... | collective-permute-start | bytes 14155784 | tf_op jit(solution)/shard_map/ppermute | solution.py:32
  317.4 4.8 copy-start.5
  319.9 200.2 %collective-permute-start.2 = (f32[2,768,6,128]{3,1,2,0:T(8,128)}, f32[2,768,6,128]{3,1,2,0:T(8,128)}, u32[]{:S(2)}, u32[]{:S(2)}) collective-permute-start(f32[2,768,6,128]{3,1,2,0:T(8,128)} %pad_maximum_fusion.1), channel_id=1, source_target_pairs={{8,0},{16,8},{24,16},{32,24},{40,32},{48,40},{56,48},{64,56},{72,6... | collective-permute-start | bytes 14155784 | tf_op jit(solution)/shard_map/ppermute | solution.py:32
  326.0 20.9 %all-to-all-start.4 = ((bf16[8,96,768]{2,1,0:T(8,128)(2,1)}), bf16[8,96,768]{2,1,0:T(8,128)(2,1)S(1)}, u32[]{:S(2)}, u32[]{:S(2)}) async-start(bf16[8,96,768]{2,1,0:T(8,128)(2,1)} %copy.87), calls=%async_computation.4 | async-start | bytes 2359296 | tf_op jit(solution)/shard_map/all_to_all | solution.py:115
  346.8 74.1 %copy-start.1 = (bf16[8,96,768]{2,1,0:T(8,128)(2,1)}, bf16[8,96,768]{2,1,0:T(8,128)(2,1)S(1)}, u32[]{:S(2)}) copy-start(bf16[8,96,768]{2,1,0:T(8,128)(2,1)S(1)} %all-to-all-done.4) | copy-start | bytes 3538948
  346.8 182.1 %all-to-all-start.5 = ((bf16[8,96,768]{2,1,0:T(8,128)(2,1)}), bf16[8,96,768]{2,1,0:T(8,128)(2,1)}, u32[]{:S(2)}, u32[]{:S(2)}) async-start(bf16[8,96,768]{2,1,0:T(8,128)(2,1)} %all_to_all.120), calls=%async_computation.5 | async-start | bytes 2359296 | tf_op jit(solution)/shard_map/all_to_all | solution.py:116
  528.9 21.6 %all-to-all-start.7 = ((bf16[8,96,768]{2,1,0:T(8,128)(2,1)}), bf16[8,96,768]{2,1,0:T(8,128)(2,1)}, u32[]{:S(2)}, u32[]{:S(2)}) async-start(bf16[8,96,768]{2,1,0:T(8,128)(2,1)} %all_to_all.128), calls=%async_computation.7 | async-start | bytes 2359296 | tf_op jit(solution)/shard_map/all_to_all | solution.py:118
  534.0 20.1 %copy-start.2 = (bf16[8,96,768]{2,1,0:T(8,128)(2,1)S(1)}, bf16[8,96,768]{2,1,0:T(8,128)(2,1)}, u32[]{:S(2)}) copy-start(bf16[8,96,768]{2,1,0:T(8,128)(2,1)} %copy-done.1) | copy-start | bytes 3538948
  550.6 20.9 %all-to-all-start.6 = ((bf16[8,96,768]{2,1,0:T(8,128)(2,1)}), bf16[8,96,768]{2,1,0:T(8,128)(2,1)S(1)}, u32[]{:S(2)}, u32[]{:S(2)}) async-start(bf16[8,96,768]{2,1,0:T(8,128)(2,1)} %all_to_all.124), calls=%async_computation.6 | async-start | bytes 2359296 | tf_op jit(solution)/shard_map/all_to_all | solution.py:117
where the time goes:
time: 579 us; the launch traced here: 573 us
  waiting for transfers between devices  298 us (51%)
  matrix products  113 us (20%)
  local copies, waits for them, and re-layouts  55.5 us (10%)
  starting transfers between devices  43.4 us (7%)
  other arithmetic  40.8 us (7%)
  blocking collectives  20 us (3%)
    ppermute x2, waiting for transfers between devices, from_behind(): return lax.ppermute(block, axis, route)  169 us
    ppermute x1, waiting for transfers between devices, padded(): lax.ppermute(tail, axis, [(i, (i + 1) % count) for i in range(ends)])  49.4 us
    dot_general x6, matrix products, single_head(): jnp.einsum('id,jd->ij', grad_one, value_one, preferred_element_type=jnp.f...  27.5 us
    all_to_all x1, blocking collectives, per_device(): lax.all_to_all(value_rows, 'tp', split_axis=1, concat_axis=0, tiled=True)  20 us
    dot_general x6, matrix products, single_head(): jnp.einsum('ij,jd->id', prob_half, value_one, preferred_element_type=jnp....  18.7 us
    dot_general x6, matrix products, single_head(): jnp.einsum('ij,id->jd', grad_score, query_one, preferred_element_type=jnp...  18.6 us
    dot_general x6, matrix products, single_head(): jnp.einsum('id,jd->ij', query_one, key_one, preferred_element_type=jnp.fl...  18.5 us
    all_to_all x1, waiting for transfers between devices, per_device(): lax.all_to_all(key_rows, 'tp', split_axis=1, concat_axis=0, tiled=True)  17.3 us
  transfers between devices with their start and end apart: 11, of which 9 were waited for; matrix products, arithmetic and copies ran while one was open for 7% of the time, Pallas kernels for 0%

commit v1 on v0

v1 whole, which is shorter than its diff:
```python
import functools

import jax
import jax.numpy as jnp
from jax import lax
from jax.experimental import pallas as pl
from jax.experimental.pallas import tpu as pltpu
from jax.sharding import Mesh, PartitionSpec as P

DH = 128
ARRAYS = 4
TILE = 256
GROUP = ("yh", "tp")
CHAIN = ("yl", "z")
LONGEST = 768
LOG2E = 1.4426950408889634
MASKED = -1e30


def pack_kernel(q_ref, k_ref, v_ref, g_ref, o_ref):
    for j in range(o_ref.shape[0]):
        for a, ref in enumerate((q_ref, k_ref, v_ref, g_ref)):
            o_ref[j, a] = ref[:, j * DH : (j + 1) * DH]


def pack(chunk, members, arrays):
    rows = arrays[0].shape[0]
    step = 4
    steps = members // step
    spec = pl.BlockSpec((rows, step * DH), lambda i: (0, chunk * steps + i))
    size = members * ARRAYS * rows * DH
    return pl.pallas_call(
        pack_kernel,
        grid=(steps,),
        in_specs=[spec] * ARRAYS,
        out_specs=pl.BlockSpec((step, ARRAYS, rows, DH), lambda i: (i, 0, 0, 0)),
        out_shape=jax.ShapeDtypeStruct((members, ARRAYS, rows, DH), jnp.bfloat16),
        cost_estimate=pl.CostEstimate(flops=0, bytes_accessed=4 * size, transcendentals=0),
        name=f"pack{chunk}",
    )(*arrays)


def unpack_kernel(r_ref, *refs):
    outs = refs[-ARRAYS:]
    for j in range(r_ref.shape[0]):
        for a, ref in enumerate(outs):
            ref[:, j * DH : (j + 1) * DH] = r_ref[j, a]


def unpack(chunk, chunks, received, earlier):
    members, _, rows, _ = received.shape
    step = 4
    steps = members // step
    size = members * ARRAYS * rows * DH
    spec = pl.BlockSpec((rows, step * DH), lambda i: (0, chunk * steps + i))
    return pl.pallas_call(
        unpack_kernel,
        grid=(steps,),
        in_specs=[pl.BlockSpec((step, ARRAYS, rows, DH), lambda i: (i, 0, 0, 0))]
        + [pl.BlockSpec(memory_space=pl.ANY)] * len(earlier),
        out_specs=[spec] * ARRAYS,
        out_shape=[jax.ShapeDtypeStruct((rows, chunks * members * DH), jnp.bfloat16)] * ARRAYS,
        input_output_aliases={1 + a: a for a in range(len(earlier))},
        cost_estimate=pl.CostEstimate(flops=0, bytes_accessed=4 * size, transcendentals=0),
        name=f"unpack{chunk}",
    )(received, *earlier)


def attend_kernel(
    lo_ref,
    hi_ref,
    qid_ref,
    kid_ref,
    own_ref,
    before_ref,
    after_ref,
    result_ref,
    to_before_ref,
    to_after_ref,
    window,
    made,
    key_t,
    value_t,
    cells,
    key_sum,
    value_sum,
    in_sems,
    out_sems,
):
    edge = before_ref.shape[0]
    members, _, part, _ = own_ref.shape
    blocks = members + 2 * edge
    length = blocks * part
    tiles = length // TILE
    scale = DH**-0.5
    places = ((0, edge), (edge, members), (edge + members, edge))
    copies = [
        pltpu.make_async_copy(
            source.at[:, a], window.at[a, pl.ds(first, count)], in_sems.at[3 * a + n]
        )
        for a in range(ARRAYS)
        for n, (source, (first, count)) in enumerate(
            zip((before_ref, own_ref, after_ref), places)
        )
    ]
    for copy in copies:
        copy.start()
    key_sum[...] = jnp.zeros_like(key_sum)
    value_sum[...] = jnp.zeros_like(value_sum)
    for copy in copies:
        copy.wait()
    rows = window.reshape(ARRAYS, length, DH)
    outs = made.reshape(ARRAYS, length, DH)

    def turn(j, carry):
        at = pl.ds(pl.multiple_of(j * TILE, TILE), TILE)
        key_t[j] = rows[1, at, :].T
        value_t[j] = rows[2, at, :].T
        return carry

    lax.fori_loop(0, tiles, turn, 0)

    def nt(a, b):
        return lax.dot_general(a, b, (((1,), (1,)), ((), ())), preferred_element_type=jnp.float32)

    def nn(a, b):
        return jnp.dot(a, b, preferred_element_type=jnp.float32)

    def query_tile(t, carry):
        at = pl.ds(pl.multiple_of(t * TILE, TILE), TILE)
        low, high = lo_ref[t], hi_ref[t]

        @pl.when(low < high)
        def _():
            query, grad = rows[0, at, :], rows[3, at, :]
            query_ids = qid_ref[pl.ds(t, 1), :]

            def scores(j, top):
                keys = pl.ds(pl.multiple_of(j * TILE, TILE), TILE)
                dots = nt(rows[1, keys, :], query)
                ids = kid_ref[keys, :]
                ids = jnp.concatenate([ids] * (TILE // DH), axis=1)
                dots = jnp.where(ids == query_ids, dots, MASKED)
                cells[keys, :] = dots
                return jnp.maximum(top, jnp.max(dots, axis=0, keepdims=True))

            top = lax.fori_loop(low, high, scores, jnp.full((1, TILE), MASKED, jnp.float32))

            def weigh(j, sums):
                total, out_t = sums
                keys = pl.ds(pl.multiple_of(j * TILE, TILE), TILE)
                weights = jnp.exp2((cells[keys, :] - top) * (scale * LOG2E))
                cells[keys, :] = weights
                total = total + jnp.sum(weights, axis=0, keepdims=True)
                return total, out_t + nn(value_t[j], weights.astype(jnp.bfloat16))

            total, out_t = lax.fori_loop(
                low,
                high,
                weigh,
                (jnp.zeros((1, TILE), jnp.float32), jnp.zeros((DH, TILE), jnp.float32)),
            )
            inverse = jnp.where(query_ids >= 0, 1.0 / total, 0.0)
            out_t = out_t * inverse
            out = out_t.T
            correction = jnp.sum(grad.astype(jnp.float32).T * out_t, axis=0, keepdims=True)
            outs[0, at, :] = out.astype(jnp.bfloat16)
            scaled = inverse * scale

            def backward(j, query_grad_t):
                keys = pl.ds(pl.multiple_of(j * TILE, TILE), TILE)
                weights = cells[keys, :]
                prob = (weights * inverse).astype(jnp.bfloat16)
                value_sum[keys, :] += nn(prob, grad)
                grad_prob = nt(rows[2, keys, :], grad)
                grad_score = (weights * scaled * (grad_prob - correction)).astype(jnp.bfloat16)
                key_sum[keys, :] += nn(grad_score, query)
                return query_grad_t + nn(key_t[j], grad_score)

            query_grad_t = lax.fori_loop(
                low, high, backward, jnp.zeros((DH, TILE), jnp.float32)
            )
            outs[1, at, :] = query_grad_t.T.astype(jnp.bfloat16)

        return carry

    lax.fori_loop(0, tiles, query_tile, 0)

    def finish(j, carry):
        at = pl.ds(pl.multiple_of(j * TILE, TILE), TILE)
        outs[2, at, :] = key_sum[at, :].astype(jnp.bfloat16)
        outs[3, at, :] = value_sum[at, :].astype(jnp.bfloat16)
        return carry

    lax.fori_loop(0, tiles, finish, 0)
    copies = [
        pltpu.make_async_copy(
            made.at[a, pl.ds(first, count)], target.at[:, a], out_sems.at[3 * a + n]
        )
        for a in range(ARRAYS)
        for n, (target, (first, count)) in enumerate(
            zip((to_before_ref, result_ref, to_after_ref), places)
        )
    ]
    for copy in copies:
        copy.start()
    for copy in copies:
        copy.wait()


def attend(chunk, plan, own, before, after):
    low, high, query_ids, key_ids = plan
    members, _, part, _ = own.shape
    edge = before.shape[0]
    blocks = members + 2 * edge
    length = blocks * part
    tiles = length // TILE
    smem = pl.BlockSpec(memory_space=pltpu.SMEM)
    vmem = pl.BlockSpec(memory_space=pltpu.VMEM)
    hbm = pl.BlockSpec(memory_space=pl.ANY)
    pairs = tiles * 4 * TILE * TILE
    return pl.pallas_call(
        attend_kernel,
        in_specs=[smem, smem, vmem, vmem, hbm, hbm, hbm],
        out_specs=[hbm, hbm, hbm],
        out_shape=[
            jax.ShapeDtypeStruct(own.shape, jnp.bfloat16),
            jax.ShapeDtypeStruct(before.shape, jnp.bfloat16),
            jax.ShapeDtypeStruct(after.shape, jnp.bfloat16),
        ],
        scratch_shapes=[
            pltpu.VMEM((ARRAYS, blocks, part, DH), jnp.bfloat16),
            pltpu.VMEM((ARRAYS, blocks, part, DH), jnp.bfloat16),
            pltpu.VMEM((tiles, DH, TILE), jnp.bfloat16),
            pltpu.VMEM((tiles, DH, TILE), jnp.bfloat16),
            pltpu.VMEM((length, TILE), jnp.float32),
            pltpu.VMEM((length, DH), jnp.float32),
            pltpu.VMEM((length, DH), jnp.float32),
            pltpu.SemaphoreType.DMA((3 * ARRAYS,)),
            pltpu.SemaphoreType.DMA((3 * ARRAYS,)),
        ],
        compiler_params=pltpu.CompilerParams(vmem_limit_bytes=40 * 1024 * 1024),
        cost_estimate=pl.CostEstimate(
            flops=12 * pairs * DH, bytes_accessed=2 * ARRAYS * 2 * length * DH, transcendentals=pairs
        ),
        name=f"attend{chunk}",
    )(low, high, query_ids, key_ids, own, before, after)


def clip_plan(clip_lengths, shard, own_rows, edge_rows):
    count = clip_lengths.shape[0]
    order = jnp.arange(count, dtype=jnp.int32)
    upto = order[:, None] >= order[None, :]
    ends = jnp.sum(jnp.where(upto, clip_lengths[None, :], 0), axis=1)
    starts = ends - clip_lengths
    first, last = starts // own_rows, (ends - 1) // own_rows
    border = last * own_rows
    owner = jnp.where((first == last) | (ends - border > border - starts), last, first)
    mine = owner == shard
    length = own_rows + 2 * edge_rows
    origin = shard * own_rows - edge_rows
    positions = origin + jnp.arange(length, dtype=jnp.int32)
    inside = mine[None, :] & (positions[:, None] >= starts[None, :]) & (positions[:, None] < ends[None, :])
    ids = jnp.sum(jnp.where(inside, order[None, :] + 1, 0), axis=1) - 1
    tiles = length // TILE
    tile_from = origin + TILE * jnp.arange(tiles, dtype=jnp.int32)[:, None]
    meets = mine[None, :] & (starts[None, :] < tile_from + TILE) & (ends[None, :] > tile_from)
    low = jnp.min(jnp.where(meets, starts[None, :] - origin, length), axis=1) // TILE
    high = (jnp.max(jnp.where(meets, ends[None, :] - origin, 0), axis=1) + TILE - 1) // TILE
    query_ids = ids.reshape(tiles, TILE)
    key_ids = jnp.broadcast_to(ids[:, None], (length, DH))
    return (low, high, query_ids, key_ids), ids >= 0


def per_device(query_rows, key_rows, value_rows, out_grad, clip_lengths):
    part, features = query_rows.shape
    members = lax.axis_size(GROUP)
    chunks = features // (members * DH)
    shards = lax.axis_size(CHAIN)
    shard = lax.axis_index(CHAIN)
    own_rows = members * part
    edge = LONGEST // 2 // part
    plan, owned = clip_plan(clip_lengths, shard, own_rows, edge * part)
    owned = owned.reshape(members + 2 * edge, 1, part, 1)
    upward = [(i, i + 1) for i in range(shards - 1)]
    downward = [(i + 1, i) for i in range(shards - 1)]

    arrays = (query_rows, key_rows, value_rows, out_grad)
    results = ()
    arrived = [
        lax.all_to_all(pack(chunk, members, arrays), GROUP, 0, 0, tiled=True)
        for chunk in range(chunks)
    ]
    leaving = []
    for chunk, own in enumerate(arrived):
        before = lax.ppermute(own[members - edge :], CHAIN, upward)
        after = lax.ppermute(own[:edge], CHAIN, downward)
        made, to_before, to_after = attend(chunk, plan, own, before, after)
        head = lax.ppermute(to_after, CHAIN, upward)
        tail = lax.ppermute(to_before, CHAIN, downward)
        made = jnp.concatenate(
            [
                jnp.where(owned[edge : 2 * edge], made[:edge], head),
                made[edge : members - edge],
                jnp.where(owned[members : members + edge], made[members - edge :], tail),
            ]
        )
        leaving.append(lax.all_to_all(made, GROUP, 0, 0, tiled=True))
    for chunk, received in enumerate(leaving):
        results = unpack(chunk, chunks, received, results)
    return tuple(results)


def solution(mesh):
    enc, ctx, tp = mesh.devices.shape
    fine = Mesh(mesh.devices.reshape(enc, ctx // 2, 2, tp), ("yl", "z", "yh", "tp"))
    rows = P(("yl", "z", "yh", "tp"), None)
    return jax.shard_map(
        per_device,
        mesh=fine,
        in_specs=(rows,) * ARRAYS + (P(),),
        out_specs=(rows,) * ARRAYS,
        check_vma=False,
    )
```

time: 579 us -> 316 us (0.55); the launches traced: 573 us -> 316 us
  waiting for transfers between devices: 298 us -> 112 us
  matrix products: 113 us -> 0 us
  Pallas kernels: 0 us -> 95.5 us
  local copies, waits for them, and re-layouts: 55.5 us -> 13.5 us
  starting transfers between devices: 43.4 us -> 84.7 us
  other arithmetic: 40.8 us -> 8.84 us
  blocking collectives: 20 us -> 0 us
    ppermute x4 -> x12, waiting for transfers between devices: 218 us -> 10.1 us  [the longest x3 6.98 us: per_device(): tail = lax.ppermute(to_before, CHAIN, downward)]
    dot_general x36 -> x0, matrix products: 113 us -> none  [the longest x6 27.5 us: single_head(): jnp.einsum('id,jd->ij', grad_one, value_one, preferred_element_type=jnp.f...]
    pallas_call x0 -> x9, Pallas kernels: none -> 95.5 us  [the longest x3 73.3 us: attend(): pl.pallas_call(attend_kernel, in_specs=[smem, smem, vmem, vmem, hbm, hbm,...]
    ppermute x4 -> x12, starting transfers between devices: 15.6 us -> 57.5 us  [the longest x3 27.9 us: per_device(): head = lax.ppermute(to_after, CHAIN, upward)]
    all_to_all x13 -> x0, local copies, waits for them, and re-layouts: 23.4 us -> none  [the longest x3 4.85 us: per_device(): lax.all_to_all(attended_heads, 'tp', split_axis=0, concat_axis=1, tiled=T...]
    all_to_all x7 -> x6, waiting for transfers between devices: 79.9 us -> 102 us  [the longest x3 58.6 us: per_device(): leaving.append(lax.all_to_all(made, GROUP, 0, 0, tiled=True))]
    convert_element_type x7 -> x0, other arithmetic: 21.2 us -> none  [the longest x6 15.3 us: single_head(): prob_half = prob_float.astype(jnp.bfloat16)]
    all_to_all x1 -> x0, blocking collectives: 20 us -> none  [per_device(): lax.all_to_all(value_rows, 'tp', split_axis=1, concat_axis=0, tiled=True)]
  transfers between devices with their start and end apart: 11 -> 18, of which waited for: 9 -> 8; matrix products, arithmetic and copies ran while one was open for 7% -> 3% of each run, Pallas kernels for 0% -> 28%
where the time goes in v1:
time: 316 us
  waiting for transfers between devices  112 us (35%)
  Pallas kernels  95.5 us (30%)
  starting transfers between devices  84.7 us (27%)
  local copies, waits for them, and re-layouts  13.5 us (4%)
  other arithmetic  8.84 us (3%)
    pallas_call x3, Pallas kernels, attend(): pl.pallas_call(attend_kernel, in_specs=[smem, smem, vmem, vmem, hbm, hbm,...  73.3 us
    all_to_all x3, waiting for transfers between devices, per_device(): leaving.append(lax.all_to_all(made, GROUP, 0, 0, tiled=True))  58.6 us
    all_to_all x3, waiting for transfers between devices, per_device(): lax.all_to_all(pack(chunk, members, arrays), GROUP, 0, 0, tiled=True)  43.2 us
    ppermute x3, starting transfers between devices, per_device(): head = lax.ppermute(to_after, CHAIN, upward)  27.9 us
    ppermute x3, starting transfers between devices, per_device(): before = lax.ppermute(own[members - edge:], CHAIN, upward)  17.4 us
    all_to_all x3, starting transfers between devices, per_device(): lax.all_to_all(pack(chunk, members, arrays), GROUP, 0, 0, tiled=True)  15.1 us
    all_to_all x3, starting transfers between devices, per_device(): leaving.append(lax.all_to_all(made, GROUP, 0, 0, tiled=True))  12 us
    pallas_call x3, Pallas kernels, pack(): pl.pallas_call(pack_kernel, grid=(steps,), in_specs=[spec] * ARRAYS, out_...  11.3 us
  transfers between devices with their start and end apart: 18, of which 8 were waited for; matrix products, arithmetic and copies ran while one was open for 3% of the time, Pallas kernels for 28%

profile of v1, /device:TPU:96, one launch (start us, length us, event | category | flops | bytes accessed | tf_op | source)
XLA Modules:
  0.0 315.5 jit_solution(14606613675667740400)
XLA Ops:
  0.6 3.8 %pack2.1 = bf16[16,4,96,128]{3,2,1,0:T(8,128)(2,1)} custom-call(bf16[96,6144]{1,0:T(8,128)(2,1)} %q_ref.5, bf16[96,6144]{1,0:T(8,128)(2,1)} %k_ref.5, bf16[96,6144]{1,0:T(8,128)(2,1)} %v_ref.5, bf16[96,6144]{1,0:T(8,128)(2,1)} %g_ref.5), custom_call_target="tpu_custom_call" | custom-call | bytes 3145728 | tf_op jit(solution)/shard_map/pack2/pallas_call | solution.py:32
  4.4 7.0 %all-to-all-start = ((bf16[16,4,96,128]{3,2,1,0:T(8,128)(2,1)}), bf16[16,4,96,128]{3,2,1,0:T(8,128)(2,1)S(1)}, u32[]{:S(2)}, u32[]{:S(2)}) async-start(bf16[16,4,96,128]{3,2,1,0:T(8,128)(2,1)} %pack2.1), calls=%async_computation | async-start | bytes 3145728 | tf_op jit(solution)/shard_map/all_to_all | solution.py:291
  11.4 3.8 %pack0.1 = bf16[16,4,96,128]{3,2,1,0:T(8,128)(2,1)} custom-call(bf16[96,6144]{1,0:T(8,128)(2,1)} %q_ref.5, bf16[96,6144]{1,0:T(8,128)(2,1)} %k_ref.5, bf16[96,6144]{1,0:T(8,128)(2,1)} %v_ref.5, bf16[96,6144]{1,0:T(8,128)(2,1)} %g_ref.5), custom_call_target="tpu_custom_call" | custom-call | bytes 3145728 | tf_op jit(solution)/shard_map/pack0/pallas_call | solution.py:32
  15.2 19.8 %all-to-all-done.own_ref = bf16[16,4,96,128]{3,2,1,0:T(8,128)(2,1)S(1)} async-done(((bf16[16,4,96,128]{3,2,1,0:T(8,128)(2,1)}), bf16[16,4,96,128]{3,2,1,0:T(8,128)(2,1)S(1)}, u32[]{:S(2)}, u32[]{:S(2)}) %all-to-all-start) | async-done | bytes 1572896 | tf_op jit(solution)/shard_map/all_to_all | solution.py:291
  35.0 3.7 %all-to-all-start.4 = ((bf16[16,4,96,128]{3,2,1,0:T(8,128)(2,1)}), bf16[16,4,96,128]{3,2,1,0:T(8,128)(2,1)S(1)}, u32[]{:S(2)}, u32[]{:S(2)}) async-start(bf16[16,4,96,128]{3,2,1,0:T(8,128)(2,1)} %pack0.1), calls=%async_computation.4 | async-start | bytes 3145728 | tf_op jit(solution)/shard_map/all_to_all | solution.py:291
  38.8 0.0 copy-start.18
  38.8 3.8 %pack1.1 = bf16[16,4,96,128]{3,2,1,0:T(8,128)(2,1)} custom-call(bf16[96,6144]{1,0:T(8,128)(2,1)} %q_ref.5, bf16[96,6144]{1,0:T(8,128)(2,1)} %k_ref.5, bf16[96,6144]{1,0:T(8,128)(2,1)} %v_ref.5, bf16[96,6144]{1,0:T(8,128)(2,1)} %g_ref.5), custom_call_target="tpu_custom_call" | custom-call | bytes 3145728 | tf_op jit(solution)/shard_map/pack1/pallas_call | solution.py:32
  42.5 0.1 select_reduce_fusion.1
  42.7 19.6 %all-to-all-done.4.own_ref = bf16[16,4,96,128]{3,2,1,0:T(8,128)(2,1)S(1)} async-done(((bf16[16,4,96,128]{3,2,1,0:T(8,128)(2,1)}), bf16[16,4,96,128]{3,2,1,0:T(8,128)(2,1)S(1)}, u32[]{:S(2)}, u32[]{:S(2)}) %all-to-all-start.4) | async-done | bytes 1572896 | tf_op jit(solution)/shard_map/all_to_all | solution.py:291
  62.3 4.4 %all-to-all-start.2 = ((bf16[16,4,96,128]{3,2,1,0:T(8,128)(2,1)}), bf16[16,4,96,128]{3,2,1,0:T(8,128)(2,1)}, u32[]{:S(2)}, u32[]{:S(2)}) async-start(bf16[16,4,96,128]{3,2,1,0:T(8,128)(2,1)} %pack1.1), calls=%async_computation.2 | async-start | bytes 3145728 | tf_op jit(solution)/shard_map/all_to_all | solution.py:291
  66.7 0.2 select_reduce_fusion
  66.9 0.6 copy-done.16
  67.5 0.2 select_reduce_fusion.2
  67.7 0.6 and_select_fusion.hi_ref
  68.3 0.5 and_select_fusion.1.lo_ref
  68.8 0.9 fusion.3
  69.8 2.3 collective-permute-start.1
  72.1 5.6 %collective-permute-start = (bf16[4,4,96,128]{3,2,1,0:T(8,128)(2,1)}, bf16[4,4,96,128]{3,2,1,0:T(8,128)(2,1)}, u32[]{:S(2)}, u32[]{:S(2)}) collective-permute-start(bf16[4,4,96,128]{3,2,1,0:T(8,128)(2,1)} %get-tuple-element.53), channel_id=1, source_target_pairs={{0,16},{16,32},{32,48},{48,64},{64,80},{80,96},{96,112},{1,17},{17... | collective-permute-start | bytes 1179656 | tf_op jit(solution)/shard_map/ppermute | solution.py:296
  77.8 0.9 fusion.1
  78.7 1.9 collective-permute-start.9
  80.6 6.0 %collective-permute-start.8 = (bf16[4,4,96,128]{3,2,1,0:T(8,128)(2,1)}, bf16[4,4,96,128]{3,2,1,0:T(8,128)(2,1)}, u32[]{:S(2)}, u32[]{:S(2)}) collective-permute-start(bf16[4,4,96,128]{3,2,1,0:T(8,128)(2,1)} %get-tuple-element.45), channel_id=1, source_target_pairs={{0,16},{16,32},{32,48},{48,64},{64,80},{80,96},{96,112},{1,17},{17... | collective-permute-start | bytes 1179656 | tf_op jit(solution)/shard_map/ppermute | solution.py:296
  86.7 3.8 %all-to-all-done.2.own_ref = bf16[16,4,96,128]{3,2,1,0:T(8,128)(2,1)} async-done(((bf16[16,4,96,128]{3,2,1,0:T(8,128)(2,1)}), bf16[16,4,96,128]{3,2,1,0:T(8,128)(2,1)}, u32[]{:S(2)}, u32[]{:S(2)}) %all-to-all-start.2) | async-done | bytes 1572896 | tf_op jit(solution)/shard_map/all_to_all | solution.py:291
  90.4 1.2 fusion.2
  91.6 2.2 collective-permute-start.5
  93.9 0.7 copy-done.4
  94.6 5.7 %collective-permute-start.4 = (bf16[4,4,96,128]{3,2,1,0:T(8,128)(2,1)S(1)}, bf16[4,4,96,128]{3,2,1,0:T(8,128)(2,1)S(1)}, u32[]{:S(2)}, u32[]{:S(2)}) collective-permute-start(bf16[4,4,96,128]{3,2,1,0:T(8,128)(2,1)S(1)} %get-tuple-element.49), channel_id=1, source_target_pairs={{0,16},{16,32},{32,48},{48,64},{64,80},{80,96},{96,112},{1,17},{17... | collective-permute-start | bytes 1179656 | tf_op jit(solution)/shard_map/ppermute | solution.py:296
  100.4 0.4 broadcast_in_dim.104.kid_ref
  100.8 1.0 copy-done.5
  101.8 24.0 %attend2.1 = (bf16[16,4,96,128]{3,2,1,0:T(8,128)(2,1)S(1)}, bf16[4,4,96,128]{3,2,1,0:T(8,128)(2,1)S(1)}, bf16[4,4,96,128]{3,2,1,0:T(8,128)(2,1)S(1)}) custom-call(s32[9]{0:T(128)S(1)} %copy-done.7, s32[9]{0:T(128)S(1)} %copy-done.6, s32[9,256]{1,0:T(8,128)S(1)} %sub.72.qid_ref, s32[2304,128]{1,0:T(8,128)S(1)} %broadcast_in_dim.104.kid_ref, ...), custom_call_target="tpu_custom_call" | custom-call | flops 3623878656 | bytes 4718592 | tf_op jit(solution)/shard_map/attend2/pallas_call | solution.py:222
  125.8 6.5 %collective-permute-start.2 = (bf16[4,4,96,128]{3,2,1,0:T(8,128)(2,1)S(1)}, bf16[4,4,96,128]{3,2,1,0:T(8,128)(2,1)S(1)}, u32[]{:S(2)}, u32[]{:S(2)}) collective-permute-start(bf16[4,4,96,128]{3,2,1,0:T(8,128)(2,1)S(1)} %get-tuple-element.22), channel_id=1, source_target_pairs={{0,16},{16,32},{32,48},{48,64},{64,80},{80,96},{96,112},{1,17},{17... | collective-permute-start | bytes 1179656 | tf_op jit(solution)/shard_map/ppermute | solution.py:299
  132.3 1.9 collective-permute-start.3
  134.2 24.6 %attend0.1 = (bf16[16,4,96,128]{3,2,1,0:T(8,128)(2,1)S(1)}, bf16[4,4,96,128]{3,2,1,0:T(8,128)(2,1)}, bf16[4,4,96,128]{3,2,1,0:T(8,128)(2,1)}) custom-call(s32[9]{0:T(128)S(1)} %copy-done.7, s32[9]{0:T(128)S(1)} %copy-done.6, s32[9,256]{1,0:T(8,128)S(1)} %sub.72.qid_ref, s32[2304,128]{1,0:T(8,128)S(1)} %broadcast_in_dim.104.kid_ref, ...), custom_call_target="tpu_custom_call" | custom-call | flops 3623878656 | bytes 4718592 | tf_op jit(solution)/shard_map/attend0/pallas_call | solution.py:222
  158.8 10.6 %collective-permute-start.10 = (bf16[4,4,96,128]{3,2,1,0:T(8,128)(2,1)}, bf16[4,4,96,128]{3,2,1,0:T(8,128)(2,1)}, u32[]{:S(2)}, u32[]{:S(2)}) collective-permute-start(bf16[4,4,96,128]{3,2,1,0:T(8,128)(2,1)} %get-tuple-element.28), channel_id=1, source_target_pairs={{0,16},{16,32},{32,48},{48,64},{64,80},{80,96},{96,112},{1,17},{17... | collective-permute-start | bytes 1179656 | tf_op jit(solution)/shard_map/ppermute | solution.py:299
  169.5 1.9 collective-permute-start.11
  171.4 24.7 %attend1.1 = (bf16[16,4,96,128]{3,2,1,0:T(8,128)(2,1)S(1)}, bf16[4,4,96,128]{3,2,1,0:T(8,128)(2,1)}, bf16[4,4,96,128]{3,2,1,0:T(8,128)(2,1)}) custom-call(s32[9]{0:T(128)S(1)} %copy-done.7, s32[9]{0:T(128)S(1)} %copy-done.6, s32[9,256]{1,0:T(8,128)S(1)} %sub.72.qid_ref, s32[2304,128]{1,0:T(8,128)S(1)} %broadcast_in_dim.104.kid_ref, ...), custom_call_target="tpu_custom_call" | custom-call | flops 3623878656 | bytes 4718592 | tf_op jit(solution)/shard_map/attend1/pallas_call | solution.py:222
  196.2 1.2 copy-done.2
  197.4 10.7 %collective-permute-start.6 = (bf16[4,4,96,128]{3,2,1,0:T(8,128)(2,1)}, bf16[4,4,96,128]{3,2,1,0:T(8,128)(2,1)}, u32[]{:S(2)}, u32[]{:S(2)}) collective-permute-start(bf16[4,4,96,128]{3,2,1,0:T(8,128)(2,1)} %get-tuple-element.25), channel_id=1, source_target_pairs={{0,16},{16,32},{32,48},{48,64},{64,80},{80,96},{96,112},{1,17},{17... | collective-permute-start | bytes 1179656 | tf_op jit(solution)/shard_map/ppermute | solution.py:299
  208.1 0.7 copy-done.13
  208.9 1.9 collective-permute-start.7
  210.8 0.7 broadcast_in_dim.98
  211.5 0.6 broadcast_in_dim.105
  212.1 0.1 slice.76
  212.2 3.1 collective-permute-done.6
  215.2 7.0 %collective-permute-done.7 = bf16[4,4,96,128]{3,2,1,0:T(8,128)(2,1)} collective-permute-done((bf16[4,4,96,128]{3,2,1,0:T(8,128)(2,1)}, bf16[4,4,96,128]{3,2,1,0:T(8,128)(2,1)}, u32[]{:S(2)}, u32[]{:S(2)}) %collective-permute-start.7) | collective-permute-done | bytes 393248 | tf_op jit(solution)/shard_map/ppermute | solution.py:300
  222.2 3.1 slice_select_fusion.5
  225.3 1.3 pad_maximum_fusion.2
  226.7 4.6 %all-to-all-start.5 = ((bf16[16,4,96,128]{3,2,1,0:T(8,128)(2,1)}), bf16[16,4,96,128]{3,2,1,0:T(8,128)(2,1)}, u32[]{:S(2)}, u32[]{:S(2)}) async-start(bf16[16,4,96,128]{3,2,1,0:T(8,128)(2,1)} %pad_maximum_fusion.2), calls=%async_computation.5 | async-start | bytes 3145728 | tf_op jit(solution)/shard_map/all_to_all | solution.py:308
  231.3 0.1 slice.71
  231.4 0.9 copy-done.11
  232.3 0.1 copy-done.12
  232.4 1.4 pad_maximum_fusion.1
  233.8 21.2 %all-to-all-done.5.r_ref = bf16[16,4,96,128]{3,2,1,0:T(8,128)(2,1)} async-done(((bf16[16,4,96,128]{3,2,1,0:T(8,128)(2,1)}), bf16[16,4,96,128]{3,2,1,0:T(8,128)(2,1)}, u32[]{:S(2)}, u32[]{:S(2)}) %all-to-all-start.5) | async-done | bytes 1572896 | tf_op jit(solution)/shard_map/all_to_all | solution.py:308
  255.0 3.7 %all-to-all-start.3 = ((bf16[16,4,96,128]{3,2,1,0:T(8,128)(2,1)}), bf16[16,4,96,128]{3,2,1,0:T(8,128)(2,1)S(1)}, u32[]{:S(2)}, u32[]{:S(2)}) async-start(bf16[16,4,96,128]{3,2,1,0:T(8,128)(2,1)} %pad_maximum_fusion.1), calls=%async_computation.3 | async-start | bytes 3145728 | tf_op jit(solution)/shard_map/all_to_all | solution.py:308
  258.7 0.1 slice.65
  258.8 0.9 copy-done.10
  259.7 1.4 pad_maximum_fusion
  261.0 21.2 %all-to-all-done.3.r_ref = bf16[16,4,96,128]{3,2,1,0:T(8,128)(2,1)S(1)} async-done(((bf16[16,4,96,128]{3,2,1,0:T(8,128)(2,1)}), bf16[16,4,96,128]{3,2,1,0:T(8,128)(2,1)S(1)}, u32[]{:S(2)}, u32[]{:S(2)}) %all-to-all-start.3) | async-done | bytes 1572896 | tf_op jit(solution)/shard_map/all_to_all | solution.py:308
  282.2 1.2 copy-done.8
  283.4 3.7 %all-to-all-start.1 = ((bf16[16,4,96,128]{3,2,1,0:T(8,128)(2,1)}), bf16[16,4,96,128]{3,2,1,0:T(8,128)(2,1)S(1)}, u32[]{:S(2)}, u32[]{:S(2)}) async-start(bf16[16,4,96,128]{3,2,1,0:T(8,128)(2,1)} %pad_maximum_fusion), calls=%async_computation.1 | async-start | bytes 3145728 | tf_op jit(solution)/shard_map/all_to_all | solution.py:308
  287.1 3.6 %unpack0.1 = (bf16[96,6144]{1,0:T(8,128)(2,1)}, bf16[96,6144]{1,0:T(8,128)(2,1)}, bf16[96,6144]{1,0:T(8,128)(2,1)}, bf16[96,6144]{1,0:T(8,128)(2,1)}) custom-call(bf16[16,4,96,128]{3,2,1,0:T(8,128)(2,1)} %all-to-all-done.5.r_ref), custom_call_target="tpu_custom_call" | custom-call | bytes 3145728 | tf_op jit(solution)/shard_map/unpack0/pallas_call | solution.py:56
  290.8 3.6 %unpack1.1 = (bf16[96,6144]{1,0:T(8,128)(2,1)}, bf16[96,6144]{1,0:T(8,128)(2,1)}, bf16[96,6144]{1,0:T(8,128)(2,1)}, bf16[96,6144]{1,0:T(8,128)(2,1)}) custom-call(bf16[16,4,96,128]{3,2,1,0:T(8,128)(2,1)} %copy-done.8, bf16[96,6144]{1,0:T(8,128)(2,1)} %get-tuple-element.30.refs_0_, ...), custom_call_target="tpu_custom_call", output_to_operand_aliasing={{0}: (1, {}), {1}: (2, {}), {2}: (3, {}), {3}: (4, {})} | custom-call | bytes 3145728 | tf_op jit(solution)/shard_map/unpack1/pallas_call | solution.py:56
  294.4 16.3 %all-to-all-done.1.r_ref = bf16[16,4,96,128]{3,2,1,0:T(8,128)(2,1)S(1)} async-done(((bf16[16,4,96,128]{3,2,1,0:T(8,128)(2,1)}), bf16[16,4,96,128]{3,2,1,0:T(8,128)(2,1)S(1)}, u32[]{:S(2)}, u32[]{:S(2)}) %all-to-all-start.1) | async-done | bytes 1572896 | tf_op jit(solution)/shard_map/all_to_all | solution.py:308
  310.7 1.2 copy-done.9
  311.9 3.6 %unpack2.1 = (bf16[96,6144]{1,0:T(8,128)(2,1)}, bf16[96,6144]{1,0:T(8,128)(2,1)}, bf16[96,6144]{1,0:T(8,128)(2,1)}, bf16[96,6144]{1,0:T(8,128)(2,1)}) custom-call(bf16[16,4,96,128]{3,2,1,0:T(8,128)(2,1)} %copy-done.9, bf16[96,6144]{1,0:T(8,128)(2,1)} %get-tuple-element.34.refs_0_, ...), custom_call_target="tpu_custom_call", output_to_operand_aliasing={{0}: (1, {}), {1}: (2, {}), {2}: (3, {}), {3}: (4, {})} | custom-call | bytes 3145728 | tf_op jit(solution)/shard_map/unpack2/pallas_call | solution.py:56
  (49 shorter events, 0.2 us)
Async XLA Ops:
  4.4 30.6 %all-to-all-start = ((bf16[16,4,96,128]{3,2,1,0:T(8,128)(2,1)}), bf16[16,4,96,128]{3,2,1,0:T(8,128)(2,1)S(1)}, u32[]{:S(2)}, u32[]{:S(2)}) async-start(bf16[16,4,96,128]{3,2,1,0:T(8,128)(2,1)} %pack2.1), calls=%async_computation | async-start | bytes 3145728 | tf_op jit(solution)/shard_map/all_to_all | solution.py:291
  35.0 27.3 %all-to-all-start.4 = ((bf16[16,4,96,128]{3,2,1,0:T(8,128)(2,1)}), bf16[16,4,96,128]{3,2,1,0:T(8,128)(2,1)S(1)}, u32[]{:S(2)}, u32[]{:S(2)}) async-start(bf16[16,4,96,128]{3,2,1,0:T(8,128)(2,1)} %pack0.1), calls=%async_computation.4 | async-start | bytes 3145728 | tf_op jit(solution)/shard_map/all_to_all | solution.py:291
  38.8 3.8 %copy-start.18 = (s32[32]{0:T(128)S(1)}, s32[32]{0:T(128)}, u32[]{:S(2)}) copy-start(s32[32]{0:T(128)} %param.9) | copy-start | bytes 388
  62.3 28.1 %all-to-all-start.2 = ((bf16[16,4,96,128]{3,2,1,0:T(8,128)(2,1)}), bf16[16,4,96,128]{3,2,1,0:T(8,128)(2,1)}, u32[]{:S(2)}, u32[]{:S(2)}) async-start(bf16[16,4,96,128]{3,2,1,0:T(8,128)(2,1)} %pack1.1), calls=%async_computation.2 | async-start | bytes 3145728 | tf_op jit(solution)/shard_map/all_to_all | solution.py:291
  66.9 0.6 copy-start.16
  67.5 2.3 copy-start.14
  69.8 24.1 %collective-permute-start.1 = (bf16[4,4,96,128]{3,2,1,0:T(8,128)(2,1)}, bf16[4,4,96,128]{3,2,1,0:T(8,128)(2,1)S(1)}, u32[]{:S(2)}, u32[]{:S(2)}) collective-permute-start(bf16[4,4,96,128]{3,2,1,0:T(8,128)(2,1)} %get-tuple-element.52), channel_id=1, source_target_pairs={{16,0},{32,16},{48,32},{64,48},{80,64},{96,80},{112,96},{17,1},{33... | collective-permute-start | bytes 1179656 | tf_op jit(solution)/shard_map/ppermute | solution.py:297
  72.1 28.3 %collective-permute-start = (bf16[4,4,96,128]{3,2,1,0:T(8,128)(2,1)}, bf16[4,4,96,128]{3,2,1,0:T(8,128)(2,1)}, u32[]{:S(2)}, u32[]{:S(2)}) collective-permute-start(bf16[4,4,96,128]{3,2,1,0:T(8,128)(2,1)} %get-tuple-element.53), channel_id=1, source_target_pairs={{0,16},{16,32},{32,48},{48,64},{64,80},{80,96},{96,112},{1,17},{17... | collective-permute-start | bytes 1179656 | tf_op jit(solution)/shard_map/ppermute | solution.py:296
  78.7 53.6 %collective-permute-start.9 = (bf16[4,4,96,128]{3,2,1,0:T(8,128)(2,1)}, bf16[4,4,96,128]{3,2,1,0:T(8,128)(2,1)}, u32[]{:S(2)}, u32[]{:S(2)}) collective-permute-start(bf16[4,4,96,128]{3,2,1,0:T(8,128)(2,1)} %get-tuple-element.44), channel_id=1, source_target_pairs={{16,0},{32,16},{48,32},{64,48},{80,64},{96,80},{112,96},{17,1},{33... | collective-permute-start | bytes 1179656 | tf_op jit(solution)/shard_map/ppermute | solution.py:297
  80.6 53.6 %collective-permute-start.8 = (bf16[4,4,96,128]{3,2,1,0:T(8,128)(2,1)}, bf16[4,4,96,128]{3,2,1,0:T(8,128)(2,1)}, u32[]{:S(2)}, u32[]{:S(2)}) collective-permute-start(bf16[4,4,96,128]{3,2,1,0:T(8,128)(2,1)} %get-tuple-element.45), channel_id=1, source_target_pairs={{0,16},{16,32},{32,48},{48,64},{64,80},{80,96},{96,112},{1,17},{17... | collective-permute-start | bytes 1179656 | tf_op jit(solution)/shard_map/ppermute | solution.py:296
  90.4 9.9 %copy-start.15 = (s32[2304]{0:T(1024)S(1)}, s32[2304]{0:T(1024)}, u32[]{:S(2)}) copy-start(s32[2304]{0:T(1024)} %copy-done.14) | copy-start | bytes 27652
  90.4 10.3 %copy-start.6 = (s32[9]{0:T(128)S(1)}, s32[9]{0:T(128)}, u32[]{:S(2)}) copy-start(s32[9]{0:T(128)} %and_select_fusion.hi_ref) | copy-start | bytes 112
  90.4 10.3 %copy-start.7 = (s32[9]{0:T(128)S(1)}, s32[9]{0:T(128)}, u32[]{:S(2)}) copy-start(s32[9]{0:T(128)} %and_select_fusion.1.lo_ref) | copy-start | bytes 112
  91.6 77.8 %collective-permute-start.5 = (bf16[4,4,96,128]{3,2,1,0:T(8,128)(2,1)S(1)}, bf16[4,4,96,128]{3,2,1,0:T(8,128)(2,1)S(1)}, u32[]{:S(2)}, u32[]{:S(2)}) collective-permute-start(bf16[4,4,96,128]{3,2,1,0:T(8,128)(2,1)S(1)} %get-tuple-element.48), channel_id=1, source_target_pairs={{16,0},{32,16},{48,32},{64,48},{80,64},{96,80},{112,96},{17,1},{33... | collective-permute-start | bytes 1179656 | tf_op jit(solution)/shard_map/ppermute | solution.py:297
  93.9 0.7 copy-start.4
  94.6 76.8 %collective-permute-start.4 = (bf16[4,4,96,128]{3,2,1,0:T(8,128)(2,1)S(1)}, bf16[4,4,96,128]{3,2,1,0:T(8,128)(2,1)S(1)}, u32[]{:S(2)}, u32[]{:S(2)}) collective-permute-start(bf16[4,4,96,128]{3,2,1,0:T(8,128)(2,1)S(1)} %get-tuple-element.49), channel_id=1, source_target_pairs={{0,16},{16,32},{32,48},{48,64},{64,80},{80,96},{96,112},{1,17},{17... | collective-permute-start | bytes 1179656 | tf_op jit(solution)/shard_map/ppermute | solution.py:296
  100.8 1.0 copy-start.5
  125.8 33.1 %copy-start = (bf16[16,4,96,128]{3,2,1,0:T(8,128)(2,1)}, bf16[16,4,96,128]{3,2,1,0:T(8,128)(2,1)S(1)}, u32[]{:S(2)}) copy-start(bf16[16,4,96,128]{3,2,1,0:T(8,128)(2,1)S(1)} %get-tuple-element.21) | copy-start | bytes 4718596
  125.8 82.4 %collective-permute-start.2 = (bf16[4,4,96,128]{3,2,1,0:T(8,128)(2,1)S(1)}, bf16[4,4,96,128]{3,2,1,0:T(8,128)(2,1)S(1)}, u32[]{:S(2)}, u32[]{:S(2)}) collective-permute-start(bf16[4,4,96,128]{3,2,1,0:T(8,128)(2,1)S(1)} %get-tuple-element.22), channel_id=1, source_target_pairs={{0,16},{16,32},{32,48},{48,64},{64,80},{80,96},{96,112},{1,17},{17... | collective-permute-start | bytes 1179656 | tf_op jit(solution)/shard_map/ppermute | solution.py:299
  132.3 79.9 %collective-permute-start.3 = (bf16[4,4,96,128]{3,2,1,0:T(8,128)(2,1)S(1)}, bf16[4,4,96,128]{3,2,1,0:T(8,128)(2,1)}, u32[]{:S(2)}, u32[]{:S(2)}) collective-permute-start(bf16[4,4,96,128]{3,2,1,0:T(8,128)(2,1)S(1)} %get-tuple-element.23), channel_id=1, source_target_pairs={{16,0},{32,16},{48,32},{64,48},{80,64},{96,80},{112,96},{17,1},{33... | collective-permute-start | bytes 1179656 | tf_op jit(solution)/shard_map/ppermute | solution.py:300
  158.8 53.3 %collective-permute-start.10 = (bf16[4,4,96,128]{3,2,1,0:T(8,128)(2,1)}, bf16[4,4,96,128]{3,2,1,0:T(8,128)(2,1)}, u32[]{:S(2)}, u32[]{:S(2)}) collective-permute-start(bf16[4,4,96,128]{3,2,1,0:T(8,128)(2,1)} %get-tuple-element.28), channel_id=1, source_target_pairs={{0,16},{16,32},{32,48},{48,64},{64,80},{80,96},{96,112},{1,17},{17... | collective-permute-start | bytes 1179656 | tf_op jit(solution)/shard_map/ppermute | solution.py:299
  169.5 41.3 %copy-start.17 = (s32[2304]{0:T(1024)S(1)}, s32[2304]{0:T(1024)}, u32[]{:S(2)}) copy-start(s32[2304]{0:T(1024)} %copy-done.16) | copy-start | bytes 27652
  169.5 42.7 %collective-permute-start.11 = (bf16[4,4,96,128]{3,2,1,0:T(8,128)(2,1)}, bf16[4,4,96,128]{3,2,1,0:T(8,128)(2,1)}, u32[]{:S(2)}, u32[]{:S(2)}) collective-permute-start(bf16[4,4,96,128]{3,2,1,0:T(8,128)(2,1)} %get-tuple-element.29), channel_id=1, source_target_pairs={{16,0},{32,16},{48,32},{64,48},{80,64},{96,80},{112,96},{17,1},{33... | collective-permute-start | bytes 1179656 | tf_op jit(solution)/shard_map/ppermute | solution.py:300
  196.2 1.2 copy-start.2
  197.4 24.9 %copy-start.1 = (bf16[16,4,96,128]{3,2,1,0:T(8,128)(2,1)S(1)}, bf16[16,4,96,128]{3,2,1,0:T(8,128)(2,1)}, u32[]{:S(2)}) copy-start(bf16[16,4,96,128]{3,2,1,0:T(8,128)(2,1)} %copy-done) | copy-start | bytes 4718596
  197.4 17.9 %collective-permute-start.6 = (bf16[4,4,96,128]{3,2,1,0:T(8,128)(2,1)}, bf16[4,4,96,128]{3,2,1,0:T(8,128)(2,1)}, u32[]{:S(2)}, u32[]{:S(2)}) collective-permute-start(bf16[4,4,96,128]{3,2,1,0:T(8,128)(2,1)} %get-tuple-element.25), channel_id=1, source_target_pairs={{0,16},{16,32},{32,48},{48,64},{64,80},{80,96},{96,112},{1,17},{17... | collective-permute-start | bytes 1179656 | tf_op jit(solution)/shard_map/ppermute | solution.py:299
  208.1 0.7 copy-start.13
  208.9 13.3 %collective-permute-start.7 = (bf16[4,4,96,128]{3,2,1,0:T(8,128)(2,1)}, bf16[4,4,96,128]{3,2,1,0:T(8,128)(2,1)}, u32[]{:S(2)}, u32[]{:S(2)}) collective-permute-start(bf16[4,4,96,128]{3,2,1,0:T(8,128)(2,1)} %get-tuple-element.26), channel_id=1, source_target_pairs={{16,0},{32,16},{48,32},{64,48},{80,64},{96,80},{112,96},{17,1},{33... | collective-permute-start | bytes 1179656 | tf_op jit(solution)/shard_map/ppermute | solution.py:300
  212.1 10.1 %copy-start.19 = (pred[4,96]{1,0:T(4,128)(4,1)S(1)}, pred[4,96]{1,0:T(4,128)(4,1)}, u32[]{:S(2)}) copy-start(pred[4,96]{1,0:T(4,128)(4,1)} %broadcast_in_dim.98) | copy-start | bytes 1156
  212.1 10.1 %copy-start.20 = (pred[4,96]{1,0:T(4,128)(4,1)S(1)}, pred[4,96]{1,0:T(4,128)(4,1)}, u32[]{:S(2)}) copy-start(pred[4,96]{1,0:T(4,128)(4,1)} %broadcast_in_dim.105) | copy-start | bytes 1156
  226.7 4.6 %copy-start.3 = (bf16[16,4,96,128]{3,2,1,0:T(8,128)(2,1)S(1)}, bf16[16,4,96,128]{3,2,1,0:T(8,128)(2,1)}, u32[]{:S(2)}) copy-start(bf16[16,4,96,128]{3,2,1,0:T(8,128)(2,1)} %copy-done.2) | copy-start | bytes 4718596
  226.7 28.3 %all-to-all-start.5 = ((bf16[16,4,96,128]{3,2,1,0:T(8,128)(2,1)}), bf16[16,4,96,128]{3,2,1,0:T(8,128)(2,1)}, u32[]{:S(2)}, u32[]{:S(2)}) async-start(bf16[16,4,96,128]{3,2,1,0:T(8,128)(2,1)} %pad_maximum_fusion.2), calls=%async_computation.5 | async-start | bytes 3145728 | tf_op jit(solution)/shard_map/all_to_all | solution.py:308
  231.3 1.0 copy-start.11
  231.3 1.1 copy-start.12
  255.0 27.3 %all-to-all-start.3 = ((bf16[16,4,96,128]{3,2,1,0:T(8,128)(2,1)}), bf16[16,4,96,128]{3,2,1,0:T(8,128)(2,1)S(1)}, u32[]{:S(2)}, u32[]{:S(2)}) async-start(bf16[16,4,96,128]{3,2,1,0:T(8,128)(2,1)} %pad_maximum_fusion.1), calls=%async_computation.3 | async-start | bytes 3145728 | tf_op jit(solution)/shard_map/all_to_all | solution.py:308
  258.7 1.0 copy-start.10
  282.2 1.2 copy-start.8
  283.4 27.3 %all-to-all-start.1 = ((bf16[16,4,96,128]{3,2,1,0:T(8,128)(2,1)}), bf16[16,4,96,128]{3,2,1,0:T(8,128)(2,1)S(1)}, u32[]{:S(2)}, u32[]{:S(2)}) async-start(bf16[16,4,96,128]{3,2,1,0:T(8,128)(2,1)} %pad_maximum_fusion), calls=%async_computation.1 | async-start | bytes 3145728 | tf_op jit(solution)/shard_map/all_to_all | solution.py:308
  310.7 1.2 copy-start.9

commit v2 on v1

--- a/solution.py
+++ b/solution.py
@@ -247,6 +247,40 @@
     )(low, high, query_ids, key_ids, own, before, after)
 
 
+def merge_kernel(kid_ref, made_ref, head_ref, tail_ref, o_ref):
+    at_head = pl.program_id(0) == 0
+    for j in range(o_ref.shape[0]):
+        mine = kid_ref[j] >= 0
+        for a in range(ARRAYS):
+            here = made_ref[j, a].astype(jnp.float32)
+            came = jnp.where(
+                at_head, head_ref[j, a].astype(jnp.float32), tail_ref[j, a].astype(jnp.float32)
+            )
+            o_ref[j, a] = jnp.where(mine, here, came).astype(jnp.bfloat16)
+
+
+def merge(chunk, plan, made, head, tail):
+    members, _, part, _ = made.shape
+    edge = head.shape[0]
+    far = members // edge - 1
+    block = (edge, ARRAYS, part, DH)
+    key_ids = plan[-1].reshape(-1, part, DH)
+    spec = pl.BlockSpec(block, lambda i: (far * i, 0, 0, 0))
+    whole = pl.BlockSpec(block, lambda i: (0, 0, 0, 0))
+    return pl.pallas_call(
+        merge_kernel,
+        grid=(2,),
+        in_specs=[pl.BlockSpec((edge, part, DH), lambda i: (1 + far * i, 0, 0)), spec, whole, whole],
+        out_specs=spec,
+        out_shape=jax.ShapeDtypeStruct(made.shape, jnp.bfloat16),
+        input_output_aliases={1: 0},
+        cost_estimate=pl.CostEstimate(
+            flops=0, bytes_accessed=12 * edge * ARRAYS * part * DH, transcendentals=0
+        ),
+        name=f"merge{chunk}",
+    )(key_ids, made, head, tail)
+
+
 def clip_plan(clip_lengths, shard, own_rows, edge_rows):
     count = clip_lengths.shape[0]
     order = jnp.arange(count, dtype=jnp.int32)
@@ -286,29 +320,49 @@
     downward = [(i + 1, i) for i in range(shards - 1)]
 
     arrays = (query_rows, key_rows, value_rows, out_grad)
-    results = ()
-    arrived = [
-        lax.all_to_all(pack(chunk, members, arrays), GROUP, 0, 0, tiled=True)
-        for chunk in range(chunks)
-    ]
-    leaving = []
-    for chunk, own in enumerate(arrived):
+    tie = lax.optimization_barrier
+    swap = functools.partial(lax.all_to_all, axis_name=GROUP, split_axis=0, concat_axis=0, tiled=True)
+
+    def compute(chunk, own):
         before = lax.ppermute(own[members - edge :], CHAIN, upward)
         after = lax.ppermute(own[:edge], CHAIN, downward)
-        made, to_before, to_after = attend(chunk, plan, own, before, after)
+        return attend(chunk, plan, own, before, after)
+
+    def settle(chunk, parts):
+        made, to_before, to_after = parts
         head = lax.ppermute(to_after, CHAIN, upward)
         tail = lax.ppermute(to_before, CHAIN, downward)
-        made = jnp.concatenate(
-            [
-                jnp.where(owned[edge : 2 * edge], made[:edge], head),
-                made[edge : members - edge],
-                jnp.where(owned[members : members + edge], made[members - edge :], tail),
-            ]
-        )
-        leaving.append(lax.all_to_all(made, GROUP, 0, 0, tiled=True))
-    for chunk, received in enumerate(leaving):
-        results = unpack(chunk, chunks, received, results)
-    return tuple(results)
+        return merge(chunk, plan, made, head, tail)
+
+    packed = [pack(chunk, members, arrays) for chunk in range(chunks)]
+    own, made, ready, got = {}, {}, {}, {}
+    own[0] = swap(packed[0])
+    for chunk in range(1, chunks):
+        if chunk >= 2:
+            packed[chunk], own[chunk - 1], made[chunk - 2] = tie(
+                (packed[chunk], own[chunk - 1], made[chunk - 2])
+            )
+            ready[chunk - 2] = settle(chunk - 2, made[chunk - 2])
+        else:
+            packed[chunk], own[chunk - 1] = tie((packed[chunk], own[chunk - 1]))
+        own[chunk] = swap(packed[chunk])
+        made[chunk - 1] = compute(chunk - 1, own[chunk - 1])
+    last = chunks - 1
+    results = ()
+    for chunk in range(chunks):
+        if chunk == 0:
+            ready[0], own[last], made[last - 1] = tie((ready[0], own[last], made[last - 1]))
+            ready[last - 1] = settle(last - 1, made[last - 1])
+            made[last] = compute(last, own[last])
+        elif chunk == 1:
+            ready[1], got[0], made[last] = tie((ready[1], got[0], made[last]))
+            ready[last] = settle(last, made[last])
+        else:
+            ready[chunk], got[chunk - 1] = tie((ready[chunk], got[chunk - 1]))
+        got[chunk] = swap(ready[chunk])
+        if chunk:
+            results = unpack(chunk - 1, chunks, got[chunk - 1], results)
+    return tuple(unpack(last, chunks, got[last], results))
 
 
 def solution(mesh):

time: 316 us -> 322 us (1.019)
  Pallas kernels: 95.5 us -> 119 us
  waiting for transfers between devices: 112 us -> 101 us
  other arithmetic: 8.84 us -> 0.55 us
  local copies, waits for them, and re-layouts: 13.5 us -> 17.6 us
    all_to_all x6, waiting for transfers between devices: 102 us -> 32 us  [the longest x3 16.3 us: per_device(): got[chunk] = swap(ready[chunk])]
    ppermute x12, waiting for transfers between devices: 10.1 us -> 69.2 us  [the longest x3 42.4 us: settle(): head = lax.ppermute(to_after, CHAIN, upward)]
    pallas_call x3, Pallas kernels: 73.3 us -> 89.9 us  [attend(): pl.pallas_call(attend_kernel, in_specs=[smem, smem, vmem, vmem, hbm, hbm,...]
    ppermute x12, starting transfers between devices: 57.5 us -> 41.5 us  [the longest x3 17.8 us: compute(): before = lax.ppermute(own[members - edge:], CHAIN, upward)]
    all_to_all x6, starting transfers between devices: 27.2 us -> 40.2 us  [the longest x3 22 us: per_device(): got[chunk] = swap(ready[chunk])]
    pallas_call x0 -> x3, Pallas kernels: none -> 7.3 us  [merge(): pl.pallas_call(merge_kernel, grid=(2,), in_specs=[pl.BlockSpec((edge, par...]
    concatenate x3 -> x0, other arithmetic: 4.08 us -> none  [per_device(): jnp.concatenate([jnp.where(owned[edge:2 * edge], made[:edge], head), made...]
    unnamed x42 -> x40, local copies, waits for them, and re-layouts: 8.59 us -> 11.9 us
  transfers between devices with their start and end apart: 18 -> 18, of which waited for: 8 -> 10; matrix products, arithmetic and copies ran while one was open for 3% -> 2% of each run, Pallas kernels for 28% -> 35%
where the time goes in v2:
time: 322 us; the launch traced here: 321 us
  Pallas kernels  119 us (37%)
  waiting for transfers between devices  101 us (31%)
  starting transfers between devices  81.7 us (25%)
  local copies, waits for them, and re-layouts  17.6 us (5%)
    pallas_call x3, Pallas kernels, attend(): pl.pallas_call(attend_kernel, in_specs=[smem, smem, vmem, vmem, hbm, hbm,...  89.9 us
    ppermute x3, waiting for transfers between devices, settle(): head = lax.ppermute(to_after, CHAIN, upward)  42.4 us
    ppermute x3, waiting for transfers between devices, compute(): after = lax.ppermute(own[:edge], CHAIN, downward)  26.3 us
    all_to_all x3, starting transfers between devices, per_device(): got[chunk] = swap(ready[chunk])  22 us
    ppermute x3, starting transfers between devices, compute(): before = lax.ppermute(own[members - edge:], CHAIN, upward)  17.8 us
    all_to_all x3, waiting for transfers between devices, per_device(): got[chunk] = swap(ready[chunk])  16.3 us
    all_to_all x1, waiting for transfers between devices, per_device(): own[0] = swap(packed[0])  15.7 us
    unnamed x40, local copies, waits for them, and re-layouts  11.9 us
  transfers between devices with their start and end apart: 18, of which 10 were waited for; matrix products, arithmetic and copies ran while one was open for 2% of the time, Pallas kernels for 35%

profile of v2, /device:TPU:96, one launch (start us, length us, event | category | flops | bytes accessed | tf_op | source)
XLA Modules:
  0.0 321.5 jit_solution(2888975481492111328)
XLA Ops:
  0.6 3.7 %pack0.1 = bf16[16,4,96,128]{3,2,1,0:T(8,128)(2,1)} custom-call(bf16[96,6144]{1,0:T(8,128)(2,1)} %q_ref.5, bf16[96,6144]{1,0:T(8,128)(2,1)} %k_ref.5, bf16[96,6144]{1,0:T(8,128)(2,1)} %v_ref.5, bf16[96,6144]{1,0:T(8,128)(2,1)} %g_ref.5), custom_call_target="tpu_custom_call" | custom-call | bytes 3145728 | tf_op jit(solution)/shard_map/pack0/pallas_call | solution.py:32
  4.4 7.0 %all-to-all-start = ((bf16[16,4,96,128]{3,2,1,0:T(8,128)(2,1)}), bf16[16,4,96,128]{3,2,1,0:T(8,128)(2,1)S(1)}, u32[]{:S(2)}, u32[]{:S(2)}) async-start(bf16[16,4,96,128]{3,2,1,0:T(8,128)(2,1)} %pack0.1), calls=%async_computation | async-start | bytes 3145728 | tf_op jit(solution)/shard_map/all_to_all | solution.py:339
  11.4 3.8 %pack2.1 = bf16[16,4,96,128]{3,2,1,0:T(8,128)(2,1)} custom-call(bf16[96,6144]{1,0:T(8,128)(2,1)} %q_ref.5, bf16[96,6144]{1,0:T(8,128)(2,1)} %k_ref.5, bf16[96,6144]{1,0:T(8,128)(2,1)} %v_ref.5, bf16[96,6144]{1,0:T(8,128)(2,1)} %g_ref.5), custom_call_target="tpu_custom_call" | custom-call | bytes 3145728 | tf_op jit(solution)/shard_map/pack2/pallas_call | solution.py:32
  15.2 3.8 %pack1.1 = bf16[16,4,96,128]{3,2,1,0:T(8,128)(2,1)} custom-call(bf16[96,6144]{1,0:T(8,128)(2,1)} %q_ref.5, bf16[96,6144]{1,0:T(8,128)(2,1)} %k_ref.5, bf16[96,6144]{1,0:T(8,128)(2,1)} %v_ref.5, bf16[96,6144]{1,0:T(8,128)(2,1)} %g_ref.5), custom_call_target="tpu_custom_call" | custom-call | bytes 3145728 | tf_op jit(solution)/shard_map/pack1/pallas_call | solution.py:32
  19.0 0.1 select_reduce_fusion.1
  19.1 0.2 select_reduce_fusion
  19.3 15.7 %all-to-all-done.own_ref = bf16[16,4,96,128]{3,2,1,0:T(8,128)(2,1)S(1)} async-done(((bf16[16,4,96,128]{3,2,1,0:T(8,128)(2,1)}), bf16[16,4,96,128]{3,2,1,0:T(8,128)(2,1)S(1)}, u32[]{:S(2)}, u32[]{:S(2)}) %all-to-all-start) | async-done | bytes 1572896 | tf_op jit(solution)/shard_map/all_to_all | solution.py:339
  35.0 3.7 %all-to-all-start.1 = ((bf16[16,4,96,128]{3,2,1,0:T(8,128)(2,1)}), bf16[16,4,96,128]{3,2,1,0:T(8,128)(2,1)S(1)}, u32[]{:S(2)}, u32[]{:S(2)}) async-start(bf16[16,4,96,128]{3,2,1,0:T(8,128)(2,1)} %pack1.1), calls=%async_computation.1 | async-start | bytes 3145728 | tf_op jit(solution)/shard_map/all_to_all | solution.py:348
  38.8 0.2 select_reduce_fusion.2
  39.0 0.1 fusion.3
  39.0 2.3 collective-permute-start.1
  41.4 5.6 %collective-permute-start = (bf16[4,4,96,128]{3,2,1,0:T(8,128)(2,1)S(1)}, bf16[4,4,96,128]{3,2,1,0:T(8,128)(2,1)S(1)}, u32[]{:S(2)}, u32[]{:S(2)}) collective-permute-start(bf16[4,4,96,128]{3,2,1,0:T(8,128)(2,1)S(1)} %get-tuple-element.85), channel_id=1, source_target_pairs={{0,16},{16,32},{32,48},{48,64},{64,80},{80,96},{96,112},{1,17},{17... | collective-permute-start | bytes 1179656 | tf_op jit(solution)/shard_map/ppermute | solution.py:327
  47.1 17.6 %collective-permute-done.1.after_ref = bf16[4,4,96,128]{3,2,1,0:T(8,128)(2,1)S(1)} collective-permute-done((bf16[4,4,96,128]{3,2,1,0:T(8,128)(2,1)S(1)}, bf16[4,4,96,128]{3,2,1,0:T(8,128)(2,1)S(1)}, u32[]{:S(2)}, u32[]{:S(2)}) %collective-permute-start.1) | collective-permute-done | bytes 393248 | tf_op jit(solution)/shard_map/ppermute | solution.py:328
  64.7 0.2 collective-permute-done.before_ref
  64.9 0.4 broadcast_in_dim.76.kid_ref
  65.3 29.8 %attend0.1 = (bf16[16,4,96,128]{3,2,1,0:T(8,128)(2,1)}, bf16[4,4,96,128]{3,2,1,0:T(8,128)(2,1)S(1)}, bf16[4,4,96,128]{3,2,1,0:T(8,128)(2,1)S(1)}) custom-call(s32[9]{0:T(128)S(1)} %and_select_fusion.1.lo_ref, s32[9]{0:T(128)S(1)} %and_select_fusion.hi_ref, s32[9,256]{1,0:T(8,128)S(1)} %sub.75.qid_ref, s32[2304,128]{1,0:T(8,128)S(1)} %broadcast_in_dim.76.kid_ref, ...), custom_call_target="tpu_custom_call" | custom-call | flops 3623878656 | bytes 4718592 | tf_op jit(solution)/shard_map/attend0/pallas_call | solution.py:222
  95.1 1.0 copy-done.1
  96.1 0.7 copy-done.4
  96.8 7.4 %all-to-all-start.2 = ((bf16[16,4,96,128]{3,2,1,0:T(8,128)(2,1)}), bf16[16,4,96,128]{3,2,1,0:T(8,128)(2,1)S(1)}, u32[]{:S(2)}, u32[]{:S(2)}) async-start(bf16[16,4,96,128]{3,2,1,0:T(8,128)(2,1)} %pack2.1), calls=%async_computation.2 | async-start | bytes 3145728 | tf_op jit(solution)/shard_map/all_to_all | solution.py:348
  104.2 1.9 collective-permute-start.2
  106.2 3.9 %collective-permute-start.3 = (bf16[4,4,96,128]{3,2,1,0:T(8,128)(2,1)S(1)}, bf16[4,4,96,128]{3,2,1,0:T(8,128)(2,1)}, u32[]{:S(2)}, u32[]{:S(2)}) collective-permute-start(bf16[4,4,96,128]{3,2,1,0:T(8,128)(2,1)S(1)} %get-tuple-element.47), channel_id=1, source_target_pairs={{16,0},{32,16},{48,32},{64,48},{80,64},{96,80},{112,96},{17,1},{33... | collective-permute-start | bytes 1179656 | tf_op jit(solution)/shard_map/ppermute | solution.py:334
  110.1 0.9 fusion.2
  111.0 1.9 collective-permute-start.5
  113.0 6.0 %collective-permute-start.4 = (bf16[4,4,96,128]{3,2,1,0:T(8,128)(2,1)}, bf16[4,4,96,128]{3,2,1,0:T(8,128)(2,1)}, u32[]{:S(2)}, u32[]{:S(2)}) collective-permute-start(bf16[4,4,96,128]{3,2,1,0:T(8,128)(2,1)} %get-tuple-element.83), channel_id=1, source_target_pairs={{0,16},{16,32},{32,48},{48,64},{64,80},{80,96},{96,112},{1,17},{17... | collective-permute-start | bytes 1179656 | tf_op jit(solution)/shard_map/ppermute | solution.py:327
  119.0 1.4 sub.68
  120.4 10.4 %collective-permute-done.2.head_ref = bf16[4,4,96,128]{3,2,1,0:T(8,128)(2,1)} collective-permute-done((bf16[4,4,96,128]{3,2,1,0:T(8,128)(2,1)}, bf16[4,4,96,128]{3,2,1,0:T(8,128)(2,1)}, u32[]{:S(2)}, u32[]{:S(2)}) %collective-permute-start.2) | collective-permute-done | bytes 393248 | tf_op jit(solution)/shard_map/ppermute | solution.py:333
  130.8 0.0 collective-permute-done.3.tail_ref
  130.9 2.0 broadcast_in_dim.71.kid_ref
  132.8 2.4 merge0.1
  135.3 3.8 %collective-permute-done.5.after_ref = bf16[4,4,96,128]{3,2,1,0:T(8,128)(2,1)} collective-permute-done((bf16[4,4,96,128]{3,2,1,0:T(8,128)(2,1)}, bf16[4,4,96,128]{3,2,1,0:T(8,128)(2,1)}, u32[]{:S(2)}, u32[]{:S(2)}) %collective-permute-start.5) | collective-permute-done | bytes 393248 | tf_op jit(solution)/shard_map/ppermute | solution.py:328
  139.1 1.3 copy-done.2
  140.4 0.6 copy-done.8
  141.0 0.6 copy-done.11
  141.6 30.5 %attend1.1 = (bf16[16,4,96,128]{3,2,1,0:T(8,128)(2,1)}, bf16[4,4,96,128]{3,2,1,0:T(8,128)(2,1)S(1)}, bf16[4,4,96,128]{3,2,1,0:T(8,128)(2,1)S(1)}) custom-call(s32[9]{0:T(128)S(1)} %copy-done.11, s32[9]{0:T(128)S(1)} %copy-done.8, s32[9,256]{1,0:T(8,128)S(1)} %sub.75.qid_ref, s32[2304,128]{1,0:T(8,128)S(1)} %copy-done.2, ...), custom_call_target="tpu_custom_call" | custom-call | flops 3623878656 | bytes 4718592 | tf_op jit(solution)/shard_map/attend1/pallas_call | solution.py:222
  172.1 0.7 copy-done.5
  172.8 7.7 %all-to-all-start.3 = ((bf16[16,4,96,128]{3,2,1,0:T(8,128)(2,1)}), bf16[16,4,96,128]{3,2,1,0:T(8,128)(2,1)}, u32[]{:S(2)}, u32[]{:S(2)}) async-start(bf16[16,4,96,128]{3,2,1,0:T(8,128)(2,1)} %merge0.1), calls=%async_computation.3 | async-start | bytes 3145728 | tf_op jit(solution)/shard_map/all_to_all | solution.py:362
  180.6 1.9 collective-permute-start.6
  182.5 3.9 %collective-permute-start.7 = (bf16[4,4,96,128]{3,2,1,0:T(8,128)(2,1)S(1)}, bf16[4,4,96,128]{3,2,1,0:T(8,128)(2,1)}, u32[]{:S(2)}, u32[]{:S(2)}) collective-permute-start(bf16[4,4,96,128]{3,2,1,0:T(8,128)(2,1)S(1)} %get-tuple-element.55), channel_id=1, source_target_pairs={{16,0},{32,16},{48,32},{64,48},{80,64},{96,80},{112,96},{17,1},{33... | collective-permute-start | bytes 1179656 | tf_op jit(solution)/shard_map/ppermute | solution.py:334
  186.4 0.9 fusion.1
  187.4 1.9 collective-permute-start.9
  189.3 6.2 %collective-permute-start.8 = (bf16[4,4,96,128]{3,2,1,0:T(8,128)(2,1)}, bf16[4,4,96,128]{3,2,1,0:T(8,128)(2,1)}, u32[]{:S(2)}, u32[]{:S(2)}) collective-permute-start(bf16[4,4,96,128]{3,2,1,0:T(8,128)(2,1)} %get-tuple-element.81), channel_id=1, source_target_pairs={{0,16},{16,32},{32,48},{48,64},{64,80},{80,96},{96,112},{1,17},{17... | collective-permute-start | bytes 1179656 | tf_op jit(solution)/shard_map/ppermute | solution.py:327
  195.5 11.5 %collective-permute-done.6.head_ref = bf16[4,4,96,128]{3,2,1,0:T(8,128)(2,1)S(1)} collective-permute-done((bf16[4,4,96,128]{3,2,1,0:T(8,128)(2,1)S(1)}, bf16[4,4,96,128]{3,2,1,0:T(8,128)(2,1)S(1)}, u32[]{:S(2)}, u32[]{:S(2)}) %collective-permute-start.6) | collective-permute-done | bytes 393248 | tf_op jit(solution)/shard_map/ppermute | solution.py:333
  207.0 0.8 copy-done.15
  207.7 2.5 merge1.1
  210.2 4.9 %collective-permute-done.9.after_ref = bf16[4,4,96,128]{3,2,1,0:T(8,128)(2,1)} collective-permute-done((bf16[4,4,96,128]{3,2,1,0:T(8,128)(2,1)}, bf16[4,4,96,128]{3,2,1,0:T(8,128)(2,1)}, u32[]{:S(2)}, u32[]{:S(2)}) %collective-permute-start.9) | collective-permute-done | bytes 393248 | tf_op jit(solution)/shard_map/ppermute | solution.py:328
  215.1 0.2 collective-permute-done.8.before_ref
  215.3 0.6 copy-done.9
  216.0 0.6 copy-done.12
  216.5 29.7 %attend2.1 = (bf16[16,4,96,128]{3,2,1,0:T(8,128)(2,1)S(1)}, bf16[4,4,96,128]{3,2,1,0:T(8,128)(2,1)S(1)}, bf16[4,4,96,128]{3,2,1,0:T(8,128)(2,1)S(1)}) custom-call(s32[9]{0:T(128)S(1)} %copy-done.12, s32[9]{0:T(128)S(1)} %copy-done.9, s32[9,256]{1,0:T(8,128)S(1)} %sub.75.qid_ref, s32[2304,128]{1,0:T(8,128)S(1)} %copy-done.3, ...), custom_call_target="tpu_custom_call" | custom-call | flops 3623878656 | bytes 4718592 | tf_op jit(solution)/shard_map/attend2/pallas_call | solution.py:222
  246.2 1.2 copy-done
  247.4 7.3 %all-to-all-start.4 = ((bf16[16,4,96,128]{3,2,1,0:T(8,128)(2,1)}), bf16[16,4,96,128]{3,2,1,0:T(8,128)(2,1)S(1)}, u32[]{:S(2)}, u32[]{:S(2)}) async-start(bf16[16,4,96,128]{3,2,1,0:T(8,128)(2,1)} %merge1.1), calls=%async_computation.4 | async-start | bytes 3145728 | tf_op jit(solution)/shard_map/all_to_all | solution.py:362
  254.7 1.9 collective-permute-start.10
  256.7 3.9 %collective-permute-start.11 = (bf16[4,4,96,128]{3,2,1,0:T(8,128)(2,1)S(1)}, bf16[4,4,96,128]{3,2,1,0:T(8,128)(2,1)S(1)}, u32[]{:S(2)}, u32[]{:S(2)}) collective-permute-start(bf16[4,4,96,128]{3,2,1,0:T(8,128)(2,1)S(1)} %get-tuple-element.63), channel_id=1, source_target_pairs={{16,0},{32,16},{48,32},{64,48},{80,64},{96,80},{112,96},{17,1},{33... | collective-permute-start | bytes 1179656 | tf_op jit(solution)/shard_map/ppermute | solution.py:334
  260.6 20.4 %collective-permute-done.10.head_ref = bf16[4,4,96,128]{3,2,1,0:T(8,128)(2,1)S(1)} collective-permute-done((bf16[4,4,96,128]{3,2,1,0:T(8,128)(2,1)S(1)}, bf16[4,4,96,128]{3,2,1,0:T(8,128)(2,1)S(1)}, u32[]{:S(2)}, u32[]{:S(2)}) %collective-permute-start.10) | collective-permute-done | bytes 393248 | tf_op jit(solution)/shard_map/ppermute | solution.py:333
  281.1 0.7 copy-done.16
  281.8 0.7 copy-done.17
  282.5 2.4 merge2.1
  285.0 1.2 copy-done.13
  286.1 7.0 %all-to-all-start.5 = ((bf16[16,4,96,128]{3,2,1,0:T(8,128)(2,1)}), bf16[16,4,96,128]{3,2,1,0:T(8,128)(2,1)S(1)}, u32[]{:S(2)}, u32[]{:S(2)}) async-start(bf16[16,4,96,128]{3,2,1,0:T(8,128)(2,1)} %merge2.1), calls=%async_computation.5 | async-start | bytes 3145728 | tf_op jit(solution)/shard_map/all_to_all | solution.py:362
  293.1 3.6 %unpack0.1 = (bf16[96,6144]{1,0:T(8,128)(2,1)}, bf16[96,6144]{1,0:T(8,128)(2,1)}, bf16[96,6144]{1,0:T(8,128)(2,1)}, bf16[96,6144]{1,0:T(8,128)(2,1)}) custom-call(bf16[16,4,96,128]{3,2,1,0:T(8,128)(2,1)} %all-to-all-done.3.r_ref), custom_call_target="tpu_custom_call" | custom-call | bytes 3145728 | tf_op jit(solution)/shard_map/unpack0/pallas_call | solution.py:56
  296.7 3.6 %unpack1.1 = (bf16[96,6144]{1,0:T(8,128)(2,1)}, bf16[96,6144]{1,0:T(8,128)(2,1)}, bf16[96,6144]{1,0:T(8,128)(2,1)}, bf16[96,6144]{1,0:T(8,128)(2,1)}) custom-call(bf16[16,4,96,128]{3,2,1,0:T(8,128)(2,1)} %copy-done.13, bf16[96,6144]{1,0:T(8,128)(2,1)} %get-tuple-element.68.refs_0_, ...), custom_call_target="tpu_custom_call", output_to_operand_aliasing={{0}: (1, {}), {1}: (2, {}), {2}: (3, {}), {3}: (4, {})} | custom-call | bytes 3145728 | tf_op jit(solution)/shard_map/unpack1/pallas_call | solution.py:56
  300.4 16.3 %all-to-all-done.5.r_ref = bf16[16,4,96,128]{3,2,1,0:T(8,128)(2,1)S(1)} async-done(((bf16[16,4,96,128]{3,2,1,0:T(8,128)(2,1)}), bf16[16,4,96,128]{3,2,1,0:T(8,128)(2,1)S(1)}, u32[]{:S(2)}, u32[]{:S(2)}) %all-to-all-start.5) | async-done | bytes 1572896 | tf_op jit(solution)/shard_map/all_to_all | solution.py:362
  316.7 1.2 copy-done.14
  317.9 3.6 %unpack2.1 = (bf16[96,6144]{1,0:T(8,128)(2,1)}, bf16[96,6144]{1,0:T(8,128)(2,1)}, bf16[96,6144]{1,0:T(8,128)(2,1)}, bf16[96,6144]{1,0:T(8,128)(2,1)}) custom-call(bf16[16,4,96,128]{3,2,1,0:T(8,128)(2,1)} %copy-done.14, bf16[96,6144]{1,0:T(8,128)(2,1)} %get-tuple-element.72.refs_0_, ...), custom_call_target="tpu_custom_call", output_to_operand_aliasing={{0}: (1, {}), {1}: (2, {}), {2}: (3, {}), {3}: (4, {})} | custom-call | bytes 3145728 | tf_op jit(solution)/shard_map/unpack2/pallas_call | solution.py:56
  (41 shorter events, 0.2 us)
Async XLA Ops:
  4.4 30.6 %all-to-all-start = ((bf16[16,4,96,128]{3,2,1,0:T(8,128)(2,1)}), bf16[16,4,96,128]{3,2,1,0:T(8,128)(2,1)S(1)}, u32[]{:S(2)}, u32[]{:S(2)}) async-start(bf16[16,4,96,128]{3,2,1,0:T(8,128)(2,1)} %pack0.1), calls=%async_computation | async-start | bytes 3145728 | tf_op jit(solution)/shard_map/all_to_all | solution.py:339
  15.2 3.8 %copy-start.19 = (s32[32]{0:T(128)S(1)}, s32[32]{0:T(128)}, u32[]{:S(2)}) copy-start(s32[32]{0:T(128)} %param.9) | copy-start | bytes 388
  35.0 61.8 %all-to-all-start.1 = ((bf16[16,4,96,128]{3,2,1,0:T(8,128)(2,1)}), bf16[16,4,96,128]{3,2,1,0:T(8,128)(2,1)S(1)}, u32[]{:S(2)}, u32[]{:S(2)}) async-start(bf16[16,4,96,128]{3,2,1,0:T(8,128)(2,1)} %pack1.1), calls=%async_computation.1 | async-start | bytes 3145728 | tf_op jit(solution)/shard_map/all_to_all | solution.py:348
  38.7 26.2 %copy-start.18 = (s32[2304]{0:T(1024)}, s32[2304]{0:T(1024)S(1)}, u32[]{:S(2)}) copy-start(s32[2304]{0:T(1024)S(1)} %broadcast_add_fusion) | copy-start | bytes 27652
  39.0 25.6 %collective-permute-start.1 = (bf16[4,4,96,128]{3,2,1,0:T(8,128)(2,1)S(1)}, bf16[4,4,96,128]{3,2,1,0:T(8,128)(2,1)S(1)}, u32[]{:S(2)}, u32[]{:S(2)}) collective-permute-start(bf16[4,4,96,128]{3,2,1,0:T(8,128)(2,1)S(1)} %get-tuple-element.84), channel_id=1, source_target_pairs={{16,0},{32,16},{48,32},{64,48},{80,64},{96,80},{112,96},{17,1},{33... | collective-permute-start | bytes 1179656 | tf_op jit(solution)/shard_map/ppermute | solution.py:328
  41.4 23.5 %collective-permute-start = (bf16[4,4,96,128]{3,2,1,0:T(8,128)(2,1)S(1)}, bf16[4,4,96,128]{3,2,1,0:T(8,128)(2,1)S(1)}, u32[]{:S(2)}, u32[]{:S(2)}) collective-permute-start(bf16[4,4,96,128]{3,2,1,0:T(8,128)(2,1)S(1)} %get-tuple-element.85), channel_id=1, source_target_pairs={{0,16},{16,32},{32,48},{48,64},{64,80},{80,96},{96,112},{1,17},{17... | collective-permute-start | bytes 1179656 | tf_op jit(solution)/shard_map/ppermute | solution.py:327
  47.0 18.3 %copy-start.7 = (s32[9]{0:T(128)}, s32[9]{0:T(128)S(1)}, u32[]{:S(2)}) copy-start(s32[9]{0:T(128)S(1)} %and_select_fusion.hi_ref) | copy-start | bytes 112
  47.0 18.2 %copy-start.10 = (s32[9]{0:T(128)}, s32[9]{0:T(128)S(1)}, u32[]{:S(2)}) copy-start(s32[9]{0:T(128)S(1)} %and_select_fusion.1.lo_ref) | copy-start | bytes 112
  95.1 1.0 copy-start.1
  96.1 0.7 copy-start.4
  96.8 76.0 %all-to-all-start.2 = ((bf16[16,4,96,128]{3,2,1,0:T(8,128)(2,1)}), bf16[16,4,96,128]{3,2,1,0:T(8,128)(2,1)S(1)}, u32[]{:S(2)}, u32[]{:S(2)}) async-start(bf16[16,4,96,128]{3,2,1,0:T(8,128)(2,1)} %pack2.1), calls=%async_computation.2 | async-start | bytes 3145728 | tf_op jit(solution)/shard_map/all_to_all | solution.py:348
  104.2 26.6 %collective-permute-start.2 = (bf16[4,4,96,128]{3,2,1,0:T(8,128)(2,1)}, bf16[4,4,96,128]{3,2,1,0:T(8,128)(2,1)}, u32[]{:S(2)}, u32[]{:S(2)}) collective-permute-start(bf16[4,4,96,128]{3,2,1,0:T(8,128)(2,1)} %copy-done.4), channel_id=1, source_target_pairs={{0,16},{16,32},{32,48},{48,64},{64,80},{80,96},{96,112},{1,17},{17... | collective-permute-start | bytes 1179656 | tf_op jit(solution)/shard_map/ppermute | solution.py:333
  106.2 24.7 %collective-permute-start.3 = (bf16[4,4,96,128]{3,2,1,0:T(8,128)(2,1)S(1)}, bf16[4,4,96,128]{3,2,1,0:T(8,128)(2,1)}, u32[]{:S(2)}, u32[]{:S(2)}) collective-permute-start(bf16[4,4,96,128]{3,2,1,0:T(8,128)(2,1)S(1)} %get-tuple-element.47), channel_id=1, source_target_pairs={{16,0},{32,16},{48,32},{64,48},{80,64},{96,80},{112,96},{17,1},{33... | collective-permute-start | bytes 1179656 | tf_op jit(solution)/shard_map/ppermute | solution.py:334
  111.0 28.1 %collective-permute-start.5 = (bf16[4,4,96,128]{3,2,1,0:T(8,128)(2,1)}, bf16[4,4,96,128]{3,2,1,0:T(8,128)(2,1)}, u32[]{:S(2)}, u32[]{:S(2)}) collective-permute-start(bf16[4,4,96,128]{3,2,1,0:T(8,128)(2,1)} %get-tuple-element.82), channel_id=1, source_target_pairs={{16,0},{32,16},{48,32},{64,48},{80,64},{96,80},{112,96},{17,1},{33... | collective-permute-start | bytes 1179656 | tf_op jit(solution)/shard_map/ppermute | solution.py:328
  113.0 26.1 %collective-permute-start.4 = (bf16[4,4,96,128]{3,2,1,0:T(8,128)(2,1)}, bf16[4,4,96,128]{3,2,1,0:T(8,128)(2,1)}, u32[]{:S(2)}, u32[]{:S(2)}) collective-permute-start(bf16[4,4,96,128]{3,2,1,0:T(8,128)(2,1)} %get-tuple-element.83), channel_id=1, source_target_pairs={{0,16},{16,32},{32,48},{48,64},{64,80},{80,96},{96,112},{1,17},{17... | collective-permute-start | bytes 1179656 | tf_op jit(solution)/shard_map/ppermute | solution.py:327
  139.1 1.3 copy-start.2
  140.4 0.6 copy-start.8
  141.0 0.6 copy-start.11
  172.1 0.7 copy-start.5
  172.8 7.8 %copy-start.6 = (bf16[4,4,96,128]{3,2,1,0:T(8,128)(2,1)S(1)}, bf16[4,4,96,128]{3,2,1,0:T(8,128)(2,1)}, u32[]{:S(2)}) copy-start(bf16[4,4,96,128]{3,2,1,0:T(8,128)(2,1)} %copy-done.5) | copy-start | bytes 1179652
  172.8 74.6 %all-to-all-start.3 = ((bf16[16,4,96,128]{3,2,1,0:T(8,128)(2,1)}), bf16[16,4,96,128]{3,2,1,0:T(8,128)(2,1)}, u32[]{:S(2)}, u32[]{:S(2)}) async-start(bf16[16,4,96,128]{3,2,1,0:T(8,128)(2,1)} %merge0.1), calls=%async_computation.3 | async-start | bytes 3145728 | tf_op jit(solution)/shard_map/all_to_all | solution.py:362
  180.6 26.4 %collective-permute-start.6 = (bf16[4,4,96,128]{3,2,1,0:T(8,128)(2,1)S(1)}, bf16[4,4,96,128]{3,2,1,0:T(8,128)(2,1)S(1)}, u32[]{:S(2)}, u32[]{:S(2)}) collective-permute-start(bf16[4,4,96,128]{3,2,1,0:T(8,128)(2,1)S(1)} %copy-done.6), channel_id=1, source_target_pairs={{0,16},{16,32},{32,48},{48,64},{64,80},{80,96},{96,112},{1,17},{17... | collective-permute-start | bytes 1179656 | tf_op jit(solution)/shard_map/ppermute | solution.py:333
  182.5 25.3 %collective-permute-start.7 = (bf16[4,4,96,128]{3,2,1,0:T(8,128)(2,1)S(1)}, bf16[4,4,96,128]{3,2,1,0:T(8,128)(2,1)}, u32[]{:S(2)}, u32[]{:S(2)}) collective-permute-start(bf16[4,4,96,128]{3,2,1,0:T(8,128)(2,1)S(1)} %get-tuple-element.55), channel_id=1, source_target_pairs={{16,0},{32,16},{48,32},{64,48},{80,64},{96,80},{112,96},{17,1},{33... | collective-permute-start | bytes 1179656 | tf_op jit(solution)/shard_map/ppermute | solution.py:334
  187.4 27.7 %collective-permute-start.9 = (bf16[4,4,96,128]{3,2,1,0:T(8,128)(2,1)}, bf16[4,4,96,128]{3,2,1,0:T(8,128)(2,1)}, u32[]{:S(2)}, u32[]{:S(2)}) collective-permute-start(bf16[4,4,96,128]{3,2,1,0:T(8,128)(2,1)} %get-tuple-element.80), channel_id=1, source_target_pairs={{16,0},{32,16},{48,32},{64,48},{80,64},{96,80},{112,96},{17,1},{33... | collective-permute-start | bytes 1179656 | tf_op jit(solution)/shard_map/ppermute | solution.py:328
  189.3 26.0 %copy-start.3 = (s32[2304,128]{1,0:T(8,128)S(1)}, s32[2304,128]{1,0:T(8,128)}, u32[]{:S(2)}) copy-start(s32[2304,128]{1,0:T(8,128)} %copy-done.1) | copy-start | bytes 3538948
  189.3 26.0 %collective-permute-start.8 = (bf16[4,4,96,128]{3,2,1,0:T(8,128)(2,1)}, bf16[4,4,96,128]{3,2,1,0:T(8,128)(2,1)}, u32[]{:S(2)}, u32[]{:S(2)}) collective-permute-start(bf16[4,4,96,128]{3,2,1,0:T(8,128)(2,1)} %get-tuple-element.81), channel_id=1, source_target_pairs={{0,16},{16,32},{32,48},{48,64},{64,80},{80,96},{96,112},{1,17},{17... | collective-permute-start | bytes 1179656 | tf_op jit(solution)/shard_map/ppermute | solution.py:327
  207.0 0.8 copy-start.15
  215.3 0.6 copy-start.9
  216.0 0.6 copy-start.12
  246.2 1.2 copy-start
  247.4 37.6 %all-to-all-start.4 = ((bf16[16,4,96,128]{3,2,1,0:T(8,128)(2,1)}), bf16[16,4,96,128]{3,2,1,0:T(8,128)(2,1)S(1)}, u32[]{:S(2)}, u32[]{:S(2)}) async-start(bf16[16,4,96,128]{3,2,1,0:T(8,128)(2,1)} %merge1.1), calls=%async_computation.4 | async-start | bytes 3145728 | tf_op jit(solution)/shard_map/all_to_all | solution.py:362
  254.7 26.3 %collective-permute-start.10 = (bf16[4,4,96,128]{3,2,1,0:T(8,128)(2,1)S(1)}, bf16[4,4,96,128]{3,2,1,0:T(8,128)(2,1)S(1)}, u32[]{:S(2)}, u32[]{:S(2)}) collective-permute-start(bf16[4,4,96,128]{3,2,1,0:T(8,128)(2,1)S(1)} %get-tuple-element.62), channel_id=1, source_target_pairs={{0,16},{16,32},{32,48},{48,64},{64,80},{80,96},{96,112},{1,17},{17... | collective-permute-start | bytes 1179656 | tf_op jit(solution)/shard_map/ppermute | solution.py:333
  256.7 24.4 %collective-permute-start.11 = (bf16[4,4,96,128]{3,2,1,0:T(8,128)(2,1)S(1)}, bf16[4,4,96,128]{3,2,1,0:T(8,128)(2,1)S(1)}, u32[]{:S(2)}, u32[]{:S(2)}) collective-permute-start(bf16[4,4,96,128]{3,2,1,0:T(8,128)(2,1)S(1)} %get-tuple-element.63), channel_id=1, source_target_pairs={{16,0},{32,16},{48,32},{64,48},{80,64},{96,80},{112,96},{17,1},{33... | collective-permute-start | bytes 1179656 | tf_op jit(solution)/shard_map/ppermute | solution.py:334
  281.0 0.7 copy-start.16
  281.8 0.7 copy-start.17
  285.0 1.2 copy-start.13
  286.1 30.6 %all-to-all-start.5 = ((bf16[16,4,96,128]{3,2,1,0:T(8,128)(2,1)}), bf16[16,4,96,128]{3,2,1,0:T(8,128)(2,1)S(1)}, u32[]{:S(2)}, u32[]{:S(2)}) async-start(bf16[16,4,96,128]{3,2,1,0:T(8,128)(2,1)} %merge2.1), calls=%async_computation.5 | async-start | bytes 3145728 | tf_op jit(solution)/shard_map/all_to_all | solution.py:362
  316.7 1.2 copy-start.14

commit v3 on v2

--- a/solution.py
+++ b/solution.py
@@ -10,6 +10,7 @@
 DH = 128
 ARRAYS = 4
 TILE = 256
+WIDTHS = (2, 3, 4, 5, 6, 8)
 GROUP = ("yh", "tp")
 CHAIN = ("yl", "z")
 LONGEST = 768
@@ -114,8 +115,8 @@
 
     def turn(j, carry):
         at = pl.ds(pl.multiple_of(j * TILE, TILE), TILE)
-        key_t[j] = rows[1, at, :].T
-        value_t[j] = rows[2, at, :].T
+        key_t[:, at] = rows[1, at, :].T
+        value_t[:, at] = rows[2, at, :].T
         return carry
 
     lax.fori_loop(0, tiles, turn, 0)
@@ -126,69 +127,47 @@
     def nn(a, b):
         return jnp.dot(a, b, preferred_element_type=jnp.float32)
 
-    def query_tile(t, carry):
+    def query_tile(t, nothing):
         at = pl.ds(pl.multiple_of(t * TILE, TILE), TILE)
-        low, high = lo_ref[t], hi_ref[t]
-
-        @pl.when(low < high)
-        def _():
+        low, count = lo_ref[t], hi_ref[t] - lo_ref[t]
+
+        def tile_of(width):
+            size = width * TILE
+            first = jnp.minimum(low, tiles - width) * TILE
+            keys = pl.ds(pl.multiple_of(first, TILE), size)
             query, grad = rows[0, at, :], rows[3, at, :]
             query_ids = qid_ref[pl.ds(t, 1), :]
-
-            def scores(j, top):
-                keys = pl.ds(pl.multiple_of(j * TILE, TILE), TILE)
-                dots = nt(rows[1, keys, :], query)
-                ids = kid_ref[keys, :]
-                ids = jnp.concatenate([ids] * (TILE // DH), axis=1)
-                dots = jnp.where(ids == query_ids, dots, MASKED)
-                cells[keys, :] = dots
-                return jnp.maximum(top, jnp.max(dots, axis=0, keepdims=True))
-
-            top = lax.fori_loop(low, high, scores, jnp.full((1, TILE), MASKED, jnp.float32))
-
-            def weigh(j, sums):
-                total, out_t = sums
-                keys = pl.ds(pl.multiple_of(j * TILE, TILE), TILE)
-                weights = jnp.exp2((cells[keys, :] - top) * (scale * LOG2E))
-                cells[keys, :] = weights
-                total = total + jnp.sum(weights, axis=0, keepdims=True)
-                return total, out_t + nn(value_t[j], weights.astype(jnp.bfloat16))
-
-            total, out_t = lax.fori_loop(
-                low,
-                high,
-                weigh,
-                (jnp.zeros((1, TILE), jnp.float32), jnp.zeros((DH, TILE), jnp.float32)),
-            )
+            dots = nt(rows[1, keys, :], query)
+            ids = kid_ref[keys, :]
+            ids = jnp.concatenate([ids] * (TILE // DH), axis=1)
+            dots = jnp.where(ids == query_ids, dots, MASKED)
+            top = jnp.max(dots, axis=0, keepdims=True)
+            weights = jnp.exp2((dots - top) * (scale * LOG2E))
+            total = jnp.sum(weights, axis=0, keepdims=True)
             inverse = jnp.where(query_ids >= 0, 1.0 / total, 0.0)
-            out_t = out_t * inverse
-            out = out_t.T
+            prob = weights * inverse
+            half = prob.astype(jnp.bfloat16)
+            out_t = nn(value_t[:, keys], half)
+            grad_prob = nt(rows[2, keys, :], grad)
             correction = jnp.sum(grad.astype(jnp.float32).T * out_t, axis=0, keepdims=True)
-            outs[0, at, :] = out.astype(jnp.bfloat16)
-            scaled = inverse * scale
-
-            def backward(j, query_grad_t):
-                keys = pl.ds(pl.multiple_of(j * TILE, TILE), TILE)
-                weights = cells[keys, :]
-                prob = (weights * inverse).astype(jnp.bfloat16)
-                value_sum[keys, :] += nn(prob, grad)
-                grad_prob = nt(rows[2, keys, :], grad)
-                grad_score = (weights * scaled * (grad_prob - correction)).astype(jnp.bfloat16)
-                key_sum[keys, :] += nn(grad_score, query)
-                return query_grad_t + nn(key_t[j], grad_score)
-
-            query_grad_t = lax.fori_loop(
-                low, high, backward, jnp.zeros((DH, TILE), jnp.float32)
-            )
-            outs[1, at, :] = query_grad_t.T.astype(jnp.bfloat16)
-
-        return carry
+            outs[0, at, :] = out_t.T.astype(jnp.bfloat16)
+            value_sum[keys, :] += nn(half, grad)
+            grad_dots = (prob * (grad_prob - correction)).astype(jnp.bfloat16)
+            key_sum[keys, :] += nn(grad_dots, query)
+            query_grad_t = nn(key_t[:, keys], grad_dots)
+            outs[1, at, :] = (query_grad_t * scale).T.astype(jnp.bfloat16)
+
+        smaller = 0
+        for width in WIDTHS:
+            pl.when((count > smaller) & (count <= width))(functools.partial(tile_of, width))
+            smaller = width
+        return nothing
 
     lax.fori_loop(0, tiles, query_tile, 0)
 
     def finish(j, carry):
         at = pl.ds(pl.multiple_of(j * TILE, TILE), TILE)
-        outs[2, at, :] = key_sum[at, :].astype(jnp.bfloat16)
+        outs[2, at, :] = (key_sum[at, :] * scale).astype(jnp.bfloat16)
         outs[3, at, :] = value_sum[at, :].astype(jnp.bfloat16)
         return carry
 
@@ -231,8 +210,8 @@
         scratch_shapes=[
             pltpu.VMEM((ARRAYS, blocks, part, DH), jnp.bfloat16),
             pltpu.VMEM((ARRAYS, blocks, part, DH), jnp.bfloat16),
-            pltpu.VMEM((tiles, DH, TILE), jnp.bfloat16),
-            pltpu.VMEM((tiles, DH, TILE), jnp.bfloat16),
+            pltpu.VMEM((DH, length), jnp.bfloat16),
+            pltpu.VMEM((DH, length), jnp.bfloat16),
             pltpu.VMEM((length, TILE), jnp.float32),
             pltpu.VMEM((length, DH), jnp.float32),
             pltpu.VMEM((length, DH), jnp.float32),
@@ -250,7 +229,8 @@
 def merge_kernel(kid_ref, made_ref, head_ref, tail_ref, o_ref):
     at_head = pl.program_id(0) == 0
     for j in range(o_ref.shape[0]):
-        mine = kid_ref[j] >= 0
+        part = o_ref.shape[2]
+        mine = kid_ref[j * part : (j + 1) * part] >= 0
         for a in range(ARRAYS):
             here = made_ref[j, a].astype(jnp.float32)
             came = jnp.where(
@@ -264,13 +244,13 @@
     edge = head.shape[0]
     far = members // edge - 1
     block = (edge, ARRAYS, part, DH)
-    key_ids = plan[-1].reshape(-1, part, DH)
+    key_ids = plan[-1]
     spec = pl.BlockSpec(block, lambda i: (far * i, 0, 0, 0))
     whole = pl.BlockSpec(block, lambda i: (0, 0, 0, 0))
     return pl.pallas_call(
         merge_kernel,
         grid=(2,),
-        in_specs=[pl.BlockSpec((edge, part, DH), lambda i: (1 + far * i, 0, 0)), spec, whole, whole],
+        in_specs=[pl.BlockSpec((edge * part, DH), lambda i: (1 + far * i, 0)), spec, whole, whole],
         out_specs=spec,
         out_shape=jax.ShapeDtypeStruct(made.shape, jnp.bfloat16),
         input_output_aliases={1: 0},
@@ -323,45 +303,52 @@
     tie = lax.optimization_barrier
     swap = functools.partial(lax.all_to_all, axis_name=GROUP, split_axis=0, concat_axis=0, tiled=True)
 
-    def compute(chunk, own):
-        before = lax.ppermute(own[members - edge :], CHAIN, upward)
-        after = lax.ppermute(own[:edge], CHAIN, downward)
-        return attend(chunk, plan, own, before, after)
-
-    def settle(chunk, parts):
+    def around(own):
+        return (
+            lax.ppermute(own[members - edge :], CHAIN, upward),
+            lax.ppermute(own[:edge], CHAIN, downward),
+        )
+
+    def back(parts):
         made, to_before, to_after = parts
         head = lax.ppermute(to_after, CHAIN, upward)
-        tail = lax.ppermute(to_before, CHAIN, downward)
-        return merge(chunk, plan, made, head, tail)
+        return made, head, lax.ppermute(to_before, CHAIN, downward)
 
     packed = [pack(chunk, members, arrays) for chunk in range(chunks)]
-    own, made, ready, got = {}, {}, {}, {}
-    own[0] = swap(packed[0])
-    for chunk in range(1, chunks):
+    last = chunks - 1
+    own, halo, made, sent, ready, got = {}, {}, {}, {}, {}, {}
+    for chunk in range(chunks):
         if chunk >= 2:
-            packed[chunk], own[chunk - 1], made[chunk - 2] = tie(
-                (packed[chunk], own[chunk - 1], made[chunk - 2])
+            packed[chunk], own[chunk - 1], halo[chunk - 2] = tie(
+                (packed[chunk], own[chunk - 1], halo[chunk - 2])
             )
-            ready[chunk - 2] = settle(chunk - 2, made[chunk - 2])
-        else:
+        elif chunk:
             packed[chunk], own[chunk - 1] = tie((packed[chunk], own[chunk - 1]))
         own[chunk] = swap(packed[chunk])
-        made[chunk - 1] = compute(chunk - 1, own[chunk - 1])
-    last = chunks - 1
+        if chunk:
+            halo[chunk - 1] = around(own[chunk - 1])
+    halo[last] = around(own[last])
+    for chunk in range(chunks):
+        inputs = (own[chunk], halo[chunk])
+        if chunk == 0:
+            inputs, own[1] = tie((inputs, own[1]))
+        elif chunk < last:
+            inputs, made[chunk - 1], own[chunk + 1] = tie((inputs, made[chunk - 1], own[chunk + 1]))
+        else:
+            inputs, ready[chunk - 2] = tie((inputs, ready[chunk - 2]))
+            got[0] = swap(ready[0])
+        made[chunk] = attend(chunk, plan, inputs[0], *inputs[1])
+        if chunk:
+            sent[chunk - 1], made[chunk] = tie((sent[chunk - 1], made[chunk]))
+            ready[chunk - 1] = merge(chunk - 1, plan, *sent[chunk - 1])
+        sent[chunk] = back(made[chunk])
     results = ()
-    for chunk in range(chunks):
-        if chunk == 0:
-            ready[0], own[last], made[last - 1] = tie((ready[0], own[last], made[last - 1]))
-            ready[last - 1] = settle(last - 1, made[last - 1])
-            made[last] = compute(last, own[last])
-        elif chunk == 1:
-            ready[1], got[0], made[last] = tie((ready[1], got[0], made[last]))
-            ready[last] = settle(last, made[last])
-        else:
-            ready[chunk], got[chunk - 1] = tie((ready[chunk], got[chunk - 1]))
+    for chunk in range(1, chunks):
+        if chunk == last:
+            ready[last] = merge(last, plan, *sent[last])
+        ready[chunk], got[chunk - 1] = tie((ready[chunk], got[chunk - 1]))
         got[chunk] = swap(ready[chunk])
-        if chunk:
-            results = unpack(chunk - 1, chunks, got[chunk - 1], results)
+        results = unpack(chunk - 1, chunks, got[chunk - 1], results)
     return tuple(unpack(last, chunks, got[last], results))
 
 

time: 322 us -> 256 us (0.80)
  Pallas kernels: 119 us -> 78.5 us
  waiting for transfers between devices: 101 us -> 71.7 us
    pallas_call x3, Pallas kernels: 89.9 us -> 49 us  [attend(): pl.pallas_call(attend_kernel, in_specs=[smem, smem, vmem, vmem, hbm, hbm,...]
    ppermute x12, waiting for transfers between devices: 69.2 us -> 35.6 us  [the longest x3 19.8 us: back(): head = lax.ppermute(to_after, CHAIN, upward)]
    all_to_all x2 -> x3, waiting for transfers between devices: 0.01 us -> 19.8 us  [per_device(): own[chunk] = swap(packed[chunk])]
    all_to_all x1, waiting for transfers between devices: 15.7 us -> 0.01 us  [per_device(): got[0] = swap(ready[0])]
    all_to_all x3 -> x2, starting transfers between devices: 22 us -> 14.5 us  [per_device(): got[chunk] = swap(ready[chunk])]
    all_to_all x2 -> x3, starting transfers between devices: 11.1 us -> 18.1 us  [per_device(): own[chunk] = swap(packed[chunk])]
    unnamed x40 -> x54, local copies, waits for them, and re-layouts: 11.9 us -> 12.2 us
    all_to_all x3 -> x2, waiting for transfers between devices: 16.3 us -> 16.3 us  [per_device(): got[chunk] = swap(ready[chunk])]
  transfers between devices with their start and end apart: 18 -> 18, of which waited for: 10 -> 7; matrix products, arithmetic and copies ran while one was open for 2% -> 3% of each run, Pallas kernels for 35% -> 28%
where the time goes in v3:
time: 256 us; the launch traced here: 254 us
  starting transfers between devices  83.9 us (33%)
  Pallas kernels  78.5 us (31%)
  waiting for transfers between devices  71.7 us (28%)
  local copies, waits for them, and re-layouts  16.5 us (6%)
    pallas_call x3, Pallas kernels, attend(): pl.pallas_call(attend_kernel, in_specs=[smem, smem, vmem, vmem, hbm, hbm,...  49 us
    ppermute x3, waiting for transfers between devices, back(): head = lax.ppermute(to_after, CHAIN, upward)  19.8 us
    all_to_all x3, waiting for transfers between devices, per_device(): own[chunk] = swap(packed[chunk])  19.8 us
    all_to_all x3, starting transfers between devices, per_device(): own[chunk] = swap(packed[chunk])  18.1 us
    ppermute x3, starting transfers between devices, around(): lax.ppermute(own[members - edge:], CHAIN, upward)  17.9 us
    all_to_all x2, waiting for transfers between devices, per_device(): got[chunk] = swap(ready[chunk])  16.3 us
    all_to_all x2, starting transfers between devices, per_device(): got[chunk] = swap(ready[chunk])  14.5 us
    unnamed x54, local copies, waits for them, and re-layouts  12.2 us
  transfers between devices with their start and end apart: 18, of which 7 were waited for; matrix products, arithmetic and copies ran while one was open for 3% of the time, Pallas kernels for 28%

profile of v3, /device:TPU:96, one launch (start us, length us, event | category | flops | bytes accessed | tf_op | source)
XLA Modules:
  0.0 254.3 jit_solution(13261414881375668963)
XLA Ops:
  0.6 3.7 %pack0.1 = bf16[16,4,96,128]{3,2,1,0:T(8,128)(2,1)} custom-call(bf16[96,6144]{1,0:T(8,128)(2,1)} %q_ref.5, bf16[96,6144]{1,0:T(8,128)(2,1)} %k_ref.5, bf16[96,6144]{1,0:T(8,128)(2,1)} %v_ref.5, bf16[96,6144]{1,0:T(8,128)(2,1)} %g_ref.5), custom_call_target="tpu_custom_call" | custom-call | bytes 3145728 | tf_op jit(solution)/shard_map/pack0/pallas_call | solution.py:33
  4.4 7.0 %all-to-all-start = ((bf16[16,4,96,128]{3,2,1,0:T(8,128)(2,1)}), bf16[16,4,96,128]{3,2,1,0:T(8,128)(2,1)S(1)}, u32[]{:S(2)}, u32[]{:S(2)}) async-start(bf16[16,4,96,128]{3,2,1,0:T(8,128)(2,1)} %pack0.1), calls=%async_computation | async-start | bytes 3145728 | tf_op jit(solution)/shard_map/all_to_all | solution.py:327
  11.4 3.8 %pack1.1 = bf16[16,4,96,128]{3,2,1,0:T(8,128)(2,1)} custom-call(bf16[96,6144]{1,0:T(8,128)(2,1)} %q_ref.5, bf16[96,6144]{1,0:T(8,128)(2,1)} %k_ref.5, bf16[96,6144]{1,0:T(8,128)(2,1)} %v_ref.5, bf16[96,6144]{1,0:T(8,128)(2,1)} %g_ref.5), custom_call_target="tpu_custom_call" | custom-call | bytes 3145728 | tf_op jit(solution)/shard_map/pack1/pallas_call | solution.py:33
  15.2 19.8 %all-to-all-done.own_ref = bf16[16,4,96,128]{3,2,1,0:T(8,128)(2,1)S(1)} async-done(((bf16[16,4,96,128]{3,2,1,0:T(8,128)(2,1)}), bf16[16,4,96,128]{3,2,1,0:T(8,128)(2,1)S(1)}, u32[]{:S(2)}, u32[]{:S(2)}) %all-to-all-start) | async-done | bytes 1572896 | tf_op jit(solution)/shard_map/all_to_all | solution.py:327
  35.0 3.7 %all-to-all-start.1 = ((bf16[16,4,96,128]{3,2,1,0:T(8,128)(2,1)}), bf16[16,4,96,128]{3,2,1,0:T(8,128)(2,1)S(1)}, u32[]{:S(2)}, u32[]{:S(2)}) async-start(bf16[16,4,96,128]{3,2,1,0:T(8,128)(2,1)} %pack1.1), calls=%async_computation.1 | async-start | bytes 3145728 | tf_op jit(solution)/shard_map/all_to_all | solution.py:327
  38.8 0.1 select_reduce_fusion.1
  38.9 0.6 broadcast_subtract_fusion.1
  39.5 0.9 fusion.3
  40.4 2.3 collective-permute-start.1
  42.7 5.6 %collective-permute-start = (bf16[4,4,96,128]{3,2,1,0:T(8,128)(2,1)}, bf16[4,4,96,128]{3,2,1,0:T(8,128)(2,1)}, u32[]{:S(2)}, u32[]{:S(2)}) collective-permute-start(bf16[4,4,96,128]{3,2,1,0:T(8,128)(2,1)} %get-tuple-element.115), channel_id=1, source_target_pairs={{0,16},{16,32},{32,48},{48,64},{64,80},{80,96},{96,112},{1,17},{17... | collective-permute-start | bytes 1179656 | tf_op jit(solution)/shard_map/ppermute | solution.py:308
  48.4 3.8 %pack2.1 = bf16[16,4,96,128]{3,2,1,0:T(8,128)(2,1)} custom-call(bf16[96,6144]{1,0:T(8,128)(2,1)} %q_ref.5, bf16[96,6144]{1,0:T(8,128)(2,1)} %k_ref.5, bf16[96,6144]{1,0:T(8,128)(2,1)} %v_ref.5, bf16[96,6144]{1,0:T(8,128)(2,1)} %g_ref.5), custom_call_target="tpu_custom_call" | custom-call | bytes 3145728 | tf_op jit(solution)/shard_map/pack2/pallas_call | solution.py:33
  52.1 0.7 fusion
  52.8 0.8 select_reduce_fusion
  53.7 0.0 copy-start.23
  53.7 0.0 copy-start.24
  53.7 11.0 %collective-permute-done.1.after_ref = bf16[4,4,96,128]{3,2,1,0:T(8,128)(2,1)S(1)} collective-permute-done((bf16[4,4,96,128]{3,2,1,0:T(8,128)(2,1)}, bf16[4,4,96,128]{3,2,1,0:T(8,128)(2,1)S(1)}, u32[]{:S(2)}, u32[]{:S(2)}) %collective-permute-start.1) | collective-permute-done | bytes 393248 | tf_op jit(solution)/shard_map/ppermute | solution.py:309
  64.7 0.3 collective-permute-done.before_ref
  65.0 0.0 all-to-all-done.1.own_ref
  65.0 7.3 %all-to-all-start.2 = ((bf16[16,4,96,128]{3,2,1,0:T(8,128)(2,1)}), bf16[16,4,96,128]{3,2,1,0:T(8,128)(2,1)}, u32[]{:S(2)}, u32[]{:S(2)}) async-start(bf16[16,4,96,128]{3,2,1,0:T(8,128)(2,1)} %pack2.1), calls=%async_computation.2 | async-start | bytes 3145728 | tf_op jit(solution)/shard_map/all_to_all | solution.py:327
  72.4 0.2 select_reduce_fusion.2
  72.7 1.0 fusion.2
  73.6 1.9 collective-permute-start.5
  75.6 6.0 %collective-permute-start.4 = (bf16[4,4,96,128]{3,2,1,0:T(8,128)(2,1)}, bf16[4,4,96,128]{3,2,1,0:T(8,128)(2,1)}, u32[]{:S(2)}, u32[]{:S(2)}) collective-permute-start(bf16[4,4,96,128]{3,2,1,0:T(8,128)(2,1)} %get-tuple-element.113), channel_id=1, source_target_pairs={{0,16},{16,32},{32,48},{48,64},{64,80},{80,96},{96,112},{1,17},{17... | collective-permute-start | bytes 1179656 | tf_op jit(solution)/shard_map/ppermute | solution.py:308
  81.6 0.4 broadcast_in_dim.69.kid_ref
  82.0 1.4 copy-done.6
  83.4 16.6 %attend0.1 = (bf16[16,4,96,128]{3,2,1,0:T(8,128)(2,1)S(1)}, bf16[4,4,96,128]{3,2,1,0:T(8,128)(2,1)}, bf16[4,4,96,128]{3,2,1,0:T(8,128)(2,1)}) custom-call(s32[9]{0:T(128)S(1)} %and_select_fusion.1.lo_ref, s32[9]{0:T(128)S(1)} %and_select_fusion.hi_ref, s32[9,256]{1,0:T(8,128)S(1)} %sub.72.qid_ref, s32[2304,128]{1,0:T(8,128)S(1)} %broadcast_in_dim.69.kid_ref, ...), custom_call_target="tpu_custom_call" | custom-call | flops 3623878656 | bytes 4718592 | tf_op jit(solution)/shard_map/attend0/pallas_call | solution.py:201
  100.0 1.2 copy-done.3
  101.2 1.9 collective-permute-start.2
  103.1 3.9 %collective-permute-start.3 = (bf16[4,4,96,128]{3,2,1,0:T(8,128)(2,1)}, bf16[4,4,96,128]{3,2,1,0:T(8,128)(2,1)}, u32[]{:S(2)}, u32[]{:S(2)}) collective-permute-start(bf16[4,4,96,128]{3,2,1,0:T(8,128)(2,1)} %get-tuple-element.65), channel_id=1, source_target_pairs={{16,0},{32,16},{48,32},{64,48},{80,64},{96,80},{112,96},{17,1},{33... | collective-permute-start | bytes 1179656 | tf_op jit(solution)/shard_map/ppermute | solution.py:315
  107.0 0.0 all-to-all-done.2.own_ref
  107.0 2.0 fusion.1
  109.1 1.9 collective-permute-start.9
  111.0 0.0 collective-permute-done.5.after_ref
  111.0 6.2 %collective-permute-start.8 = (bf16[4,4,96,128]{3,2,1,0:T(8,128)(2,1)}, bf16[4,4,96,128]{3,2,1,0:T(8,128)(2,1)S(1)}, u32[]{:S(2)}, u32[]{:S(2)}) collective-permute-start(bf16[4,4,96,128]{3,2,1,0:T(8,128)(2,1)} %get-tuple-element.111), channel_id=1, source_target_pairs={{0,16},{16,32},{32,48},{48,64},{64,80},{80,96},{96,112},{1,17},{17... | collective-permute-start | bytes 1179656 | tf_op jit(solution)/shard_map/ppermute | solution.py:308
  117.3 16.1 %attend1.1 = (bf16[16,4,96,128]{3,2,1,0:T(8,128)(2,1)S(1)}, bf16[4,4,96,128]{3,2,1,0:T(8,128)(2,1)S(1)}, bf16[4,4,96,128]{3,2,1,0:T(8,128)(2,1)S(1)}) custom-call(s32[9]{0:T(128)S(1)} %copy-done.15, s32[9]{0:T(128)S(1)} %copy-done.12, s32[9,256]{1,0:T(8,128)S(1)} %sub.72.qid_ref, s32[2304,128]{1,0:T(8,128)S(1)} %broadcast_in_dim.69.kid_ref, ...), custom_call_target="tpu_custom_call" | custom-call | flops 3623878656 | bytes 4718592 | tf_op jit(solution)/shard_map/attend1/pallas_call | solution.py:201
  133.4 1.1 copy-done.2
  134.6 0.8 copy-done.7
  135.3 0.7 copy-done.9
  136.1 2.4 merge0.1
  138.6 7.5 %all-to-all-start.3 = ((bf16[16,4,96,128]{3,2,1,0:T(8,128)(2,1)}), bf16[16,4,96,128]{3,2,1,0:T(8,128)(2,1)}, u32[]{:S(2)}, u32[]{:S(2)}) async-start(bf16[16,4,96,128]{3,2,1,0:T(8,128)(2,1)} %merge0.1), calls=%async_computation.3 | async-start | bytes 3145728 | tf_op jit(solution)/shard_map/all_to_all | solution.py:339
  146.1 1.9 collective-permute-start.6
  148.1 4.2 %collective-permute-start.7 = (bf16[4,4,96,128]{3,2,1,0:T(8,128)(2,1)S(1)}, bf16[4,4,96,128]{3,2,1,0:T(8,128)(2,1)S(1)}, u32[]{:S(2)}, u32[]{:S(2)}) collective-permute-start(bf16[4,4,96,128]{3,2,1,0:T(8,128)(2,1)S(1)} %copy-done.8), channel_id=1, source_target_pairs={{16,0},{32,16},{48,32},{64,48},{80,64},{96,80},{112,96},{17,1},{33... | collective-permute-start | bytes 1179656 | tf_op jit(solution)/shard_map/ppermute | solution.py:315
  152.2 0.6 copy-done.13
  152.8 0.6 copy-done.16
  153.5 16.3 %attend2.1 = (bf16[16,4,96,128]{3,2,1,0:T(8,128)(2,1)S(1)}, bf16[4,4,96,128]{3,2,1,0:T(8,128)(2,1)S(1)}, bf16[4,4,96,128]{3,2,1,0:T(8,128)(2,1)S(1)}) custom-call(s32[9]{0:T(128)S(1)} %copy-done.16, s32[9]{0:T(128)S(1)} %copy-done.13, s32[9,256]{1,0:T(8,128)S(1)} %sub.72.qid_ref, s32[2304,128]{1,0:T(8,128)S(1)} %copy-done.1, ...), custom_call_target="tpu_custom_call" | custom-call | flops 3623878656 | bytes 4718592 | tf_op jit(solution)/shard_map/attend2/pallas_call | solution.py:201
  169.8 1.2 copy-done.4
  171.0 1.4 collective-permute-done.6.head_ref
  172.4 0.7 copy-done.19
  173.1 0.7 copy-done.20
  173.8 2.4 merge1.1
  176.3 7.0 %all-to-all-start.4 = ((bf16[16,4,96,128]{3,2,1,0:T(8,128)(2,1)}), bf16[16,4,96,128]{3,2,1,0:T(8,128)(2,1)S(1)}, u32[]{:S(2)}, u32[]{:S(2)}) async-start(bf16[16,4,96,128]{3,2,1,0:T(8,128)(2,1)} %merge1.1), calls=%async_computation.4 | async-start | bytes 3145728 | tf_op jit(solution)/shard_map/all_to_all | solution.py:350
  183.2 5.9 %collective-permute-start.10 = (bf16[4,4,96,128]{3,2,1,0:T(8,128)(2,1)S(1)}, bf16[4,4,96,128]{3,2,1,0:T(8,128)(2,1)S(1)}, u32[]{:S(2)}, u32[]{:S(2)}) collective-permute-start(bf16[4,4,96,128]{3,2,1,0:T(8,128)(2,1)S(1)} %get-tuple-element.88), channel_id=1, source_target_pairs={{0,16},{16,32},{32,48},{48,64},{64,80},{80,96},{96,112},{1,17},{17... | collective-permute-start | bytes 1179656 | tf_op jit(solution)/shard_map/ppermute | solution.py:314
  189.1 1.9 collective-permute-start.11
  191.1 18.5 %collective-permute-done.10.head_ref = bf16[4,4,96,128]{3,2,1,0:T(8,128)(2,1)S(1)} collective-permute-done((bf16[4,4,96,128]{3,2,1,0:T(8,128)(2,1)S(1)}, bf16[4,4,96,128]{3,2,1,0:T(8,128)(2,1)S(1)}, u32[]{:S(2)}, u32[]{:S(2)}) %collective-permute-start.10) | collective-permute-done | bytes 393248 | tf_op jit(solution)/shard_map/ppermute | solution.py:314
  209.5 4.4 %collective-permute-done.11.tail_ref = bf16[4,4,96,128]{3,2,1,0:T(8,128)(2,1)S(1)} collective-permute-done((bf16[4,4,96,128]{3,2,1,0:T(8,128)(2,1)S(1)}, bf16[4,4,96,128]{3,2,1,0:T(8,128)(2,1)S(1)}, u32[]{:S(2)}, u32[]{:S(2)}) %collective-permute-start.11) | collective-permute-done | bytes 393248 | tf_op jit(solution)/shard_map/ppermute | solution.py:315
  214.0 0.7 copy-done.22
  214.7 2.4 merge2.1
  217.2 1.1 copy-done.17
  218.3 7.6 %all-to-all-start.5 = ((bf16[16,4,96,128]{3,2,1,0:T(8,128)(2,1)}), bf16[16,4,96,128]{3,2,1,0:T(8,128)(2,1)S(1)}, u32[]{:S(2)}, u32[]{:S(2)}) async-start(bf16[16,4,96,128]{3,2,1,0:T(8,128)(2,1)} %merge2.1), calls=%async_computation.5 | async-start | bytes 3145728 | tf_op jit(solution)/shard_map/all_to_all | solution.py:350
  225.9 3.6 %unpack0.1 = (bf16[96,6144]{1,0:T(8,128)(2,1)}, bf16[96,6144]{1,0:T(8,128)(2,1)}, bf16[96,6144]{1,0:T(8,128)(2,1)}, bf16[96,6144]{1,0:T(8,128)(2,1)}) custom-call(bf16[16,4,96,128]{3,2,1,0:T(8,128)(2,1)} %all-to-all-done.3.r_ref), custom_call_target="tpu_custom_call" | custom-call | bytes 3145728 | tf_op jit(solution)/shard_map/unpack0/pallas_call | solution.py:57
  229.5 3.6 %unpack1.1 = (bf16[96,6144]{1,0:T(8,128)(2,1)}, bf16[96,6144]{1,0:T(8,128)(2,1)}, bf16[96,6144]{1,0:T(8,128)(2,1)}, bf16[96,6144]{1,0:T(8,128)(2,1)}) custom-call(bf16[16,4,96,128]{3,2,1,0:T(8,128)(2,1)} %copy-done.17, bf16[96,6144]{1,0:T(8,128)(2,1)} %get-tuple-element.98.refs_0_, ...), custom_call_target="tpu_custom_call", output_to_operand_aliasing={{0}: (1, {}), {1}: (2, {}), {2}: (3, {}), {3}: (4, {})} | custom-call | bytes 3145728 | tf_op jit(solution)/shard_map/unpack1/pallas_call | solution.py:57
  233.2 16.3 %all-to-all-done.5.r_ref = bf16[16,4,96,128]{3,2,1,0:T(8,128)(2,1)S(1)} async-done(((bf16[16,4,96,128]{3,2,1,0:T(8,128)(2,1)}), bf16[16,4,96,128]{3,2,1,0:T(8,128)(2,1)S(1)}, u32[]{:S(2)}, u32[]{:S(2)}) %all-to-all-start.5) | async-done | bytes 1572896 | tf_op jit(solution)/shard_map/all_to_all | solution.py:350
  249.5 1.2 copy-done.18
  250.7 3.6 %unpack2.1 = (bf16[96,6144]{1,0:T(8,128)(2,1)}, bf16[96,6144]{1,0:T(8,128)(2,1)}, bf16[96,6144]{1,0:T(8,128)(2,1)}, bf16[96,6144]{1,0:T(8,128)(2,1)}) custom-call(bf16[16,4,96,128]{3,2,1,0:T(8,128)(2,1)} %copy-done.18, bf16[96,6144]{1,0:T(8,128)(2,1)} %get-tuple-element.102.refs_0_, ...), custom_call_target="tpu_custom_call", output_to_operand_aliasing={{0}: (1, {}), {1}: (2, {}), {2}: (3, {}), {3}: (4, {})} | custom-call | bytes 3145728 | tf_op jit(solution)/shard_map/unpack2/pallas_call | solution.py:57
  (53 shorter events, 0.1 us)
Async XLA Ops:
  4.4 30.6 %all-to-all-start = ((bf16[16,4,96,128]{3,2,1,0:T(8,128)(2,1)}), bf16[16,4,96,128]{3,2,1,0:T(8,128)(2,1)S(1)}, u32[]{:S(2)}, u32[]{:S(2)}) async-start(bf16[16,4,96,128]{3,2,1,0:T(8,128)(2,1)} %pack0.1), calls=%async_computation | async-start | bytes 3145728 | tf_op jit(solution)/shard_map/all_to_all | solution.py:327
  15.2 23.6 %copy-start.26 = (s32[32]{0:T(128)S(1)}, s32[32]{0:T(128)}, u32[]{:S(2)}) copy-start(s32[32]{0:T(128)} %param.9) | copy-start | bytes 388
  35.0 17.1 %copy-start.5 = (bf16[16,4,96,128]{3,2,1,0:T(8,128)(2,1)}, bf16[16,4,96,128]{3,2,1,0:T(8,128)(2,1)S(1)}, u32[]{:S(2)}) copy-start(bf16[16,4,96,128]{3,2,1,0:T(8,128)(2,1)S(1)} %all-to-all-done.own_ref) | copy-start | bytes 4718596
  35.0 30.0 %all-to-all-start.1 = ((bf16[16,4,96,128]{3,2,1,0:T(8,128)(2,1)}), bf16[16,4,96,128]{3,2,1,0:T(8,128)(2,1)S(1)}, u32[]{:S(2)}, u32[]{:S(2)}) async-start(bf16[16,4,96,128]{3,2,1,0:T(8,128)(2,1)} %pack1.1), calls=%async_computation.1 | async-start | bytes 3145728 | tf_op jit(solution)/shard_map/all_to_all | solution.py:327
  40.4 24.2 %collective-permute-start.1 = (bf16[4,4,96,128]{3,2,1,0:T(8,128)(2,1)}, bf16[4,4,96,128]{3,2,1,0:T(8,128)(2,1)S(1)}, u32[]{:S(2)}, u32[]{:S(2)}) collective-permute-start(bf16[4,4,96,128]{3,2,1,0:T(8,128)(2,1)} %get-tuple-element.114), channel_id=1, source_target_pairs={{16,0},{32,16},{48,32},{64,48},{80,64},{96,80},{112,96},{17,1},{33... | collective-permute-start | bytes 1179656 | tf_op jit(solution)/shard_map/ppermute | solution.py:309
  42.7 22.3 %collective-permute-start = (bf16[4,4,96,128]{3,2,1,0:T(8,128)(2,1)}, bf16[4,4,96,128]{3,2,1,0:T(8,128)(2,1)}, u32[]{:S(2)}, u32[]{:S(2)}) collective-permute-start(bf16[4,4,96,128]{3,2,1,0:T(8,128)(2,1)} %get-tuple-element.115), channel_id=1, source_target_pairs={{0,16},{16,32},{32,48},{48,64},{64,80},{80,96},{96,112},{1,17},{17... | collective-permute-start | bytes 1179656 | tf_op jit(solution)/shard_map/ppermute | solution.py:308
  53.7 18.7 %copy-start.23 = (s32[32]{0:T(128)S(1)}, s32[32]{0:T(128)}, u32[]{:S(2)}) copy-start(s32[32]{0:T(128)} %get-tuple-element.109) | copy-start | bytes 388
  53.7 18.7 %copy-start.24 = (s32[32]{0:T(128)S(1)}, s32[32]{0:T(128)}, u32[]{:S(2)}) copy-start(s32[32]{0:T(128)} %get-tuple-element.108) | copy-start | bytes 388
  53.7 18.7 %copy-start.25 = (s32[32]{0:T(128)S(1)}, s32[32]{0:T(128)}, u32[]{:S(2)}) copy-start(s32[32]{0:T(128)} %get-tuple-element.116) | copy-start | bytes 388
  65.0 42.0 %all-to-all-start.2 = ((bf16[16,4,96,128]{3,2,1,0:T(8,128)(2,1)}), bf16[16,4,96,128]{3,2,1,0:T(8,128)(2,1)}, u32[]{:S(2)}, u32[]{:S(2)}) async-start(bf16[16,4,96,128]{3,2,1,0:T(8,128)(2,1)} %pack2.1), calls=%async_computation.2 | async-start | bytes 3145728 | tf_op jit(solution)/shard_map/all_to_all | solution.py:327
  72.6 27.3 %copy-start.11 = (s32[9]{0:T(128)}, s32[9]{0:T(128)S(1)}, u32[]{:S(2)}) copy-start(s32[9]{0:T(128)S(1)} %and_select_fusion.hi_ref) | copy-start | bytes 112
  72.7 27.3 %copy-start.14 = (s32[9]{0:T(128)}, s32[9]{0:T(128)S(1)}, u32[]{:S(2)}) copy-start(s32[9]{0:T(128)S(1)} %and_select_fusion.1.lo_ref) | copy-start | bytes 112
  73.6 37.4 %collective-permute-start.5 = (bf16[4,4,96,128]{3,2,1,0:T(8,128)(2,1)}, bf16[4,4,96,128]{3,2,1,0:T(8,128)(2,1)}, u32[]{:S(2)}, u32[]{:S(2)}) collective-permute-start(bf16[4,4,96,128]{3,2,1,0:T(8,128)(2,1)} %get-tuple-element.112), channel_id=1, source_target_pairs={{16,0},{32,16},{48,32},{64,48},{80,64},{96,80},{112,96},{17,1},{33... | collective-permute-start | bytes 1179656 | tf_op jit(solution)/shard_map/ppermute | solution.py:309
  75.6 41.7 %collective-permute-start.4 = (bf16[4,4,96,128]{3,2,1,0:T(8,128)(2,1)}, bf16[4,4,96,128]{3,2,1,0:T(8,128)(2,1)}, u32[]{:S(2)}, u32[]{:S(2)}) collective-permute-start(bf16[4,4,96,128]{3,2,1,0:T(8,128)(2,1)} %get-tuple-element.113), channel_id=1, source_target_pairs={{0,16},{16,32},{32,48},{48,64},{64,80},{80,96},{96,112},{1,17},{17... | collective-permute-start | bytes 1179656 | tf_op jit(solution)/shard_map/ppermute | solution.py:308
  82.0 1.4 copy-start.6
  83.4 33.8 %copy-start = (s32[2304,128]{1,0:T(8,128)}, s32[2304,128]{1,0:T(8,128)S(1)}, u32[]{:S(2)}) copy-start(s32[2304,128]{1,0:T(8,128)S(1)} %broadcast_in_dim.69.kid_ref) | copy-start | bytes 3538948
  100.0 1.2 copy-start.3
  101.2 34.9 %collective-permute-start.2 = (bf16[4,4,96,128]{3,2,1,0:T(8,128)(2,1)}, bf16[4,4,96,128]{3,2,1,0:T(8,128)(2,1)}, u32[]{:S(2)}, u32[]{:S(2)}) collective-permute-start(bf16[4,4,96,128]{3,2,1,0:T(8,128)(2,1)} %get-tuple-element.64), channel_id=1, source_target_pairs={{0,16},{16,32},{32,48},{48,64},{64,80},{80,96},{96,112},{1,17},{17... | collective-permute-start | bytes 1179656 | tf_op jit(solution)/shard_map/ppermute | solution.py:314
  103.1 33.0 %collective-permute-start.3 = (bf16[4,4,96,128]{3,2,1,0:T(8,128)(2,1)}, bf16[4,4,96,128]{3,2,1,0:T(8,128)(2,1)}, u32[]{:S(2)}, u32[]{:S(2)}) collective-permute-start(bf16[4,4,96,128]{3,2,1,0:T(8,128)(2,1)} %get-tuple-element.65), channel_id=1, source_target_pairs={{16,0},{32,16},{48,32},{64,48},{80,64},{96,80},{112,96},{17,1},{33... | collective-permute-start | bytes 1179656 | tf_op jit(solution)/shard_map/ppermute | solution.py:315
  107.0 10.2 %copy-start.12 = (s32[9]{0:T(128)S(1)}, s32[9]{0:T(128)}, u32[]{:S(2)}) copy-start(s32[9]{0:T(128)} %copy-done.11) | copy-start | bytes 112
  107.0 10.2 %copy-start.15 = (s32[9]{0:T(128)S(1)}, s32[9]{0:T(128)}, u32[]{:S(2)}) copy-start(s32[9]{0:T(128)} %copy-done.14) | copy-start | bytes 112
  109.1 29.5 %collective-permute-start.9 = (bf16[4,4,96,128]{3,2,1,0:T(8,128)(2,1)}, bf16[4,4,96,128]{3,2,1,0:T(8,128)(2,1)S(1)}, u32[]{:S(2)}, u32[]{:S(2)}) collective-permute-start(bf16[4,4,96,128]{3,2,1,0:T(8,128)(2,1)} %get-tuple-element.110), channel_id=1, source_target_pairs={{16,0},{32,16},{48,32},{64,48},{80,64},{96,80},{112,96},{17,1},{33... | collective-permute-start | bytes 1179656 | tf_op jit(solution)/shard_map/ppermute | solution.py:309
  111.0 27.5 %collective-permute-start.8 = (bf16[4,4,96,128]{3,2,1,0:T(8,128)(2,1)}, bf16[4,4,96,128]{3,2,1,0:T(8,128)(2,1)S(1)}, u32[]{:S(2)}, u32[]{:S(2)}) collective-permute-start(bf16[4,4,96,128]{3,2,1,0:T(8,128)(2,1)} %get-tuple-element.111), channel_id=1, source_target_pairs={{0,16},{16,32},{32,48},{48,64},{64,80},{80,96},{96,112},{1,17},{17... | collective-permute-start | bytes 1179656 | tf_op jit(solution)/shard_map/ppermute | solution.py:308
  133.4 1.1 copy-start.2
  134.6 0.8 copy-start.7
  135.3 0.7 copy-start.9
  138.5 7.6 %copy-start.10 = (bf16[4,4,96,128]{3,2,1,0:T(8,128)(2,1)S(1)}, bf16[4,4,96,128]{3,2,1,0:T(8,128)(2,1)}, u32[]{:S(2)}) copy-start(bf16[4,4,96,128]{3,2,1,0:T(8,128)(2,1)} %copy-done.9) | copy-start | bytes 1179652
  138.5 9.5 %copy-start.8 = (bf16[4,4,96,128]{3,2,1,0:T(8,128)(2,1)S(1)}, bf16[4,4,96,128]{3,2,1,0:T(8,128)(2,1)}, u32[]{:S(2)}) copy-start(bf16[4,4,96,128]{3,2,1,0:T(8,128)(2,1)} %copy-done.7) | copy-start | bytes 1179652
  138.5 13.7 %copy-start.1 = (s32[2304,128]{1,0:T(8,128)S(1)}, s32[2304,128]{1,0:T(8,128)}, u32[]{:S(2)}) copy-start(s32[2304,128]{1,0:T(8,128)} %copy-done) | copy-start | bytes 3538948
  138.6 37.7 %all-to-all-start.3 = ((bf16[16,4,96,128]{3,2,1,0:T(8,128)(2,1)}), bf16[16,4,96,128]{3,2,1,0:T(8,128)(2,1)}, u32[]{:S(2)}, u32[]{:S(2)}) async-start(bf16[16,4,96,128]{3,2,1,0:T(8,128)(2,1)} %merge0.1), calls=%async_computation.3 | async-start | bytes 3145728 | tf_op jit(solution)/shard_map/all_to_all | solution.py:339
  146.1 26.2 %collective-permute-start.6 = (bf16[4,4,96,128]{3,2,1,0:T(8,128)(2,1)S(1)}, bf16[4,4,96,128]{3,2,1,0:T(8,128)(2,1)S(1)}, u32[]{:S(2)}, u32[]{:S(2)}) collective-permute-start(bf16[4,4,96,128]{3,2,1,0:T(8,128)(2,1)S(1)} %copy-done.10), channel_id=1, source_target_pairs={{0,16},{16,32},{32,48},{48,64},{64,80},{80,96},{96,112},{1,17},{17... | collective-permute-start | bytes 1179656 | tf_op jit(solution)/shard_map/ppermute | solution.py:314
  148.1 24.3 %collective-permute-start.7 = (bf16[4,4,96,128]{3,2,1,0:T(8,128)(2,1)S(1)}, bf16[4,4,96,128]{3,2,1,0:T(8,128)(2,1)S(1)}, u32[]{:S(2)}, u32[]{:S(2)}) collective-permute-start(bf16[4,4,96,128]{3,2,1,0:T(8,128)(2,1)S(1)} %copy-done.8), channel_id=1, source_target_pairs={{16,0},{32,16},{48,32},{64,48},{80,64},{96,80},{112,96},{17,1},{33... | collective-permute-start | bytes 1179656 | tf_op jit(solution)/shard_map/ppermute | solution.py:315
  152.2 0.6 copy-start.13
  152.8 0.6 copy-start.16
  169.8 1.2 copy-start.4
  172.4 0.7 copy-start.19
  173.1 0.7 copy-start.20
  176.3 40.9 %all-to-all-start.4 = ((bf16[16,4,96,128]{3,2,1,0:T(8,128)(2,1)}), bf16[16,4,96,128]{3,2,1,0:T(8,128)(2,1)S(1)}, u32[]{:S(2)}, u32[]{:S(2)}) async-start(bf16[16,4,96,128]{3,2,1,0:T(8,128)(2,1)} %merge1.1), calls=%async_computation.4 | async-start | bytes 3145728 | tf_op jit(solution)/shard_map/all_to_all | solution.py:350
  183.2 26.3 %collective-permute-start.10 = (bf16[4,4,96,128]{3,2,1,0:T(8,128)(2,1)S(1)}, bf16[4,4,96,128]{3,2,1,0:T(8,128)(2,1)S(1)}, u32[]{:S(2)}, u32[]{:S(2)}) collective-permute-start(bf16[4,4,96,128]{3,2,1,0:T(8,128)(2,1)S(1)} %get-tuple-element.88), channel_id=1, source_target_pairs={{0,16},{16,32},{32,48},{48,64},{64,80},{80,96},{96,112},{1,17},{17... | collective-permute-start | bytes 1179656 | tf_op jit(solution)/shard_map/ppermute | solution.py:314
  189.1 24.8 %collective-permute-start.11 = (bf16[4,4,96,128]{3,2,1,0:T(8,128)(2,1)S(1)}, bf16[4,4,96,128]{3,2,1,0:T(8,128)(2,1)S(1)}, u32[]{:S(2)}, u32[]{:S(2)}) collective-permute-start(bf16[4,4,96,128]{3,2,1,0:T(8,128)(2,1)S(1)} %get-tuple-element.89), channel_id=1, source_target_pairs={{16,0},{32,16},{48,32},{64,48},{80,64},{96,80},{112,96},{17,1},{33... | collective-permute-start | bytes 1179656 | tf_op jit(solution)/shard_map/ppermute | solution.py:315
  209.5 4.4 %copy-start.21 = (bf16[4,4,96,128]{3,2,1,0:T(8,128)(2,1)}, bf16[4,4,96,128]{3,2,1,0:T(8,128)(2,1)S(1)}, u32[]{:S(2)}) copy-start(bf16[4,4,96,128]{3,2,1,0:T(8,128)(2,1)S(1)} %collective-permute-done.10.head_ref) | copy-start | bytes 1179652
  214.0 0.7 copy-start.22
  217.2 1.1 copy-start.17
  218.3 31.2 %all-to-all-start.5 = ((bf16[16,4,96,128]{3,2,1,0:T(8,128)(2,1)}), bf16[16,4,96,128]{3,2,1,0:T(8,128)(2,1)S(1)}, u32[]{:S(2)}, u32[]{:S(2)}) async-start(bf16[16,4,96,128]{3,2,1,0:T(8,128)(2,1)} %merge2.1), calls=%async_computation.5 | async-start | bytes 3145728 | tf_op jit(solution)/shard_map/all_to_all | solution.py:350
  249.5 1.2 copy-start.18
